TPU v7x, 32 devices: a whole 2x2x4 slice. The times are simulated.
32 devices in a mesh: replica: 8 (over z, x), tensor: 4 (over y, core).
Axes of the slice: x: 2, y: 2, z: 4, core: 2. Of those that a mesh axis runs over, the one named last changes fastest.
Arguments:
- tokens: bfloat16 [8, 384, 2048], P('replica', 'tensor'), may hold values from -6 to 6
- targets: bfloat16 [8, 384, 2048], P('replica', 'tensor'), may hold values from -6 to 6
- gate_weight: bfloat16 [8, 2048, 7168], P('replica', None, 'tensor'), may hold values from -6 to 6
- probes: bfloat16 [8, 2048, 7168], P('replica', None, 'tensor'), may hold values from -6 to 6
- tracker: bfloat16 [8, 2048, 7168], P('replica', None, 'tensor'), may hold values from 0.049804688 to 2
- up_weight: bfloat16 [2048, 7168], P('replica', 'tensor'), may hold values from -6 to 6
- down_weight: bfloat16 [7168, 2048], P('tensor', 'replica'), may hold values from -6 to 6
- neighbours: int32 [8, 6], replicated, may hold values from 0 to 7, as said below
- numerators: int32 [8, 6], replicated, may hold values from 0 to 8, as said below
Outputs:
- mixed_weights: bfloat16 [8, 2048, 7168], P('replica', None, 'tensor')
- mixed_tracker: bfloat16 [8, 2048, 7168], P('replica', None, 'tensor')
Inputs may be any that keep to these rules, and one draw needn't show every extreme that they name: `neighbours`: every slot of row r holds r itself or a replica r - o modulo 8 with o one of 1, -1, 2, -2, 4, -4, each o at most once in a row; a row has between 2 and 6 slots that are not r, and some row has 6. `numerators`: A numerator is 0 exactly in slots that hold the row's own replica, and 4 to 8 elsewhere.
All inputs are finite; a program needn't handle non-finite values.
Results may differ from a plain program's by a relative error of at most 0.0058.
Values may be sent and summed in bfloat16 or wider, within the bound.
No kernel may reach another device: no remote copies, remote signals or barrier semaphores. Data moves between devices by JAX's collectives and lax.ppermute only.
A program may use at most 192 MiB of HBM per device.

v0:
```python
import math

import jax
import jax.numpy as jnp
from jax import lax
from jax.sharding import PartitionSpec as P

D = 2048
FF = 7168
DEN = 64


step_size = 0.1
floor_value = 0.1
tracker_decay = 0.75


def passed_along(value, axis, steps):
    count = lax.axis_size(axis)
    pairs = [(source, (source + steps) % count) for source in range(count)]
    return lax.ppermute(value, axis, pairs)


def mix_shard(shard_value, lag_of_slot, row_numer, self_weight):
    replicas_count = lax.axis_size("replica")
    mixed_sum = self_weight * shard_value.astype(jnp.float32)
    offset_list = [1, -1, 2, -2, 4]
    if replicas_count > 8:
        offset_list = offset_list + [-4]
    for offset_value in offset_list:
        received = passed_along(shard_value, "replica", offset_value)
        matched = jnp.where(lag_of_slot == offset_value % replicas_count, row_numer, 0)
        mixed_sum = mixed_sum + jnp.sum(matched).astype(jnp.float32) / DEN * received.astype(
            jnp.float32
        )
    return mixed_sum.astype(jnp.bfloat16)


def local(
    tokens, targets, gate_weight, probes, tracker, up_weight, down_weight, neighbours, numerators
):
    inv_width = 1.0 / math.sqrt(D)
    inv_hidden = 1.0 / math.sqrt(FF)
    gathered = lax.all_gather(tokens[0], "tensor", axis=0, tiled=True)
    weight_now = gate_weight[0]
    tracker_now = tracker[0]
    probe_here = probes[0]
    gate_pre = jnp.dot(gathered, weight_now, preferred_element_type=jnp.float32) * inv_width
    up_pre = (
        jnp.dot(
            gathered,
            lax.all_gather(up_weight, "replica", axis=0, tiled=True),
            preferred_element_type=jnp.float32,
        )
        * inv_width
    )
    down_full = lax.all_gather(down_weight, "replica", axis=1, tiled=True)
    logistic = jax.nn.sigmoid(gate_pre)
    activated = gate_pre * logistic
    slope_one = logistic * (1.0 + gate_pre * (1.0 - logistic))
    slope_two = logistic * (1.0 - logistic) * (2.0 + gate_pre * (1.0 - 2.0 * logistic))
    hidden = (activated * up_pre).astype(jnp.bfloat16)

    def forward_term(source):
        return jnp.dot(source, down_full, preferred_element_type=jnp.float32) * inv_hidden

    def backward_rows(shard_piece):
        return (
            lax.dot_general(
                shard_piece, down_full, (((1,), (1,)), ((), ())), preferred_element_type=jnp.float32
            )
            * inv_hidden
        )

    outputs = lax.psum_scatter(forward_term(hidden), "tensor", scatter_dimension=0, tiled=True)
    residual = (outputs - targets[0].astype(jnp.float32)).astype(jnp.bfloat16)
    grad_hidden = backward_rows(lax.all_gather(residual, "tensor", axis=0, tiled=True))
    grad_gate = (grad_hidden * up_pre * slope_one).astype(jnp.bfloat16)
    gradient = (
        lax.dot_general(
            gathered, grad_gate, (((0,), (0,)), ((), ())), preferred_element_type=jnp.float32
        )
        * inv_width
    )
    ratio = gradient / jnp.maximum(tracker_now.astype(jnp.float32), floor_value)
    stepped = (weight_now.astype(jnp.float32) - step_size * jnp.clip(ratio, -1.0, 1.0)).astype(
        jnp.bfloat16
    )
    replica_index = lax.axis_index("replica")
    row_links = neighbours[replica_index]
    row_numer = numerators[replica_index]
    lag_of_slot = jnp.mod(replica_index - row_links, lax.axis_size("replica"))
    self_weight = (DEN - jnp.sum(row_numer)).astype(jnp.float32) / DEN
    mixed_weights = mix_shard(stepped, lag_of_slot, row_numer, self_weight)
    probe_pre = jnp.dot(gathered, probe_here, preferred_element_type=jnp.float32) * inv_width
    tangent_hidden = (slope_one * probe_pre * up_pre).astype(jnp.bfloat16)
    tangent_out = lax.psum_scatter(
        forward_term(tangent_hidden), "tensor", scatter_dimension=0, tiled=True
    )
    tangent_res = tangent_out.astype(jnp.bfloat16)
    tangent_grad = backward_rows(lax.all_gather(tangent_res, "tensor", axis=0, tiled=True))
    tangent_gate = (
        (tangent_grad * slope_one + grad_hidden * slope_two * probe_pre) * up_pre
    ).astype(jnp.bfloat16)
    curvature_probe = (
        lax.dot_general(
            gathered, tangent_gate, (((0,), (0,)), ((), ())), preferred_element_type=jnp.float32
        )
        * inv_width
    )
    tracked = (
        tracker_decay * tracker_now.astype(jnp.float32)
        + (1.0 - tracker_decay) * probe_here.astype(jnp.float32) * curvature_probe
    ).astype(jnp.bfloat16)
    mixed_tracker = mix_shard(tracked, lag_of_slot, row_numer, self_weight)
    return (mixed_weights[None], mixed_tracker[None])


def solution(mesh):
    return jax.shard_map(
        local,
        mesh=mesh,
        in_specs=(
            P("replica", "tensor", None),
            P("replica", "tensor", None),
            P("replica", None, "tensor"),
            P("replica", None, "tensor"),
            P("replica", None, "tensor"),
            P("replica", "tensor"),
            P("tensor", "replica"),
            P(),
            P(),
        ),
        out_specs=(P("replica", None, "tensor"), P("replica", None, "tensor")),
        check_vma=False,
    )
```

profile of v0, /device:TPU:17, one launch (start us, length us, event | category | flops | bytes accessed | tf_op | source)
XLA Modules:
  0.0 2022.1 jit_solution(8858949878399459361)
XLA Ops:
  9.4 21.3 %all-gather.15.cloned.1.call-done = bf16[1,384,2048]{2,1,0:T(8,128)(2,1)} async-done(((bf16[1,96,2048]{2,1,0:T(8,128)(2,1)}), bf16[1,384,2048]{2,1,0:T(8,128)(2,1)}) %all-gather.15.cloned.1.call-update) | async-done | bytes 1572880 | tf_op jit(solution)/shard_map/all_gather | solution.py:44
  30.7 8.2 fusion.15
  39.0 104.3 %all-gather.7.cloned.1.call-done = bf16[2048,1792]{1,0:T(8,128)(2,1)} async-done(((bf16[256,1792]{1,0:T(8,128)(2,1)}), bf16[2048,1792]{1,0:T(8,128)(2,1)}) %all-gather.7.cloned.1.call-update) | async-done | bytes 7340048 | tf_op jit(solution)/shard_map/all_gather | solution.py:52
  150.8 105.3 %all-gather.9.cloned.1.call-done = bf16[1792,2048]{1,0:T(8,128)(2,1)} async-done(((bf16[1792,256]{1,0:T(8,128)(2,1)}), bf16[1792,2048]{1,0:T(8,128)(2,1)}) %all-gather.9.cloned.1.call-update) | async-done | bytes 7340048 | tf_op jit(solution)/shard_map/all_gather | solution.py:57
  256.1 9.5 convolution_multiply_fusion.4
  273.0 9.2 convolution_multiply_fusion.3
  282.3 20.9 %reduce-scatter.3.cloned.1.call-done = f32[96,2048]{1,0:T(8,128)} async-done(((f32[384,2048]{1,0:T(8,128)}), f32[96,2048]{1,0:T(8,128)}) %reduce-scatter.3.cloned.1.call-update) | async-done | bytes 786448 | tf_op jit(solution)/shard_map/reduce_scatter | solution.py:75
  305.5 38.9 %reduce-scatter.5.cloned.1.call-done = f32[96,2048]{1,0:T(8,128)} async-done(((f32[384,2048]{1,0:T(8,128)}), f32[96,2048]{1,0:T(8,128)}) %reduce-scatter.5.cloned.1.call-update) | async-done | bytes 786448 | tf_op jit(solution)/shard_map/reduce_scatter | solution.py:97
  346.3 10.5 copy.13
  356.8 10.5 copy.12
  375.4 11.7 all-gather.13.cloned.1.call-done
  387.1 20.5 %fusion.7 = bf16[2048,1792]{0,1:T(8,128)(2,1)} fusion(bf16[1,2048,1792]{1,2,0:T(8,128)(2,1)} %copy.12, bf16[1,2048,1792]{1,2,0:T(8,128)(2,1)} %copy.13, bf16[1,384,2048]{2,1,0:T(8,128)(2,1)S(1)} %copy-done.1, f32[384,1792]{1,0:T(8,128)} %convolution_multiply_fusion.2, bf16[384,2048]{1,0:T(8,128)(2,1)} %all-gather.13.cloned.1.call-done, ...), kind=kOutput, calls=%fused_computation.9 | convolution fusion | flops 5680267264 | bytes 43515904 | tf_op jit(solution)/shard_map/dot_general | solution.py:106
  412.4 10.4 copy.11
  422.8 15.9 fusion.8
  438.7 283.9 %collective-permute-done.9 = bf16[2048,1792]{0,1:T(8,128)(2,1)} collective-permute-done((bf16[2048,1792]{0,1:T(8,128)(2,1)}, bf16[2048,1792]{0,1:T(8,128)(2,1)}, u32[]{:S(2)}, u32[]{:S(2)}) %collective-permute-start.9) | collective-permute-done | bytes 7340064 | tf_op jit(solution)/shard_map/ppermute | solution.py:21
  725.7 311.5 %collective-permute-done.8 = bf16[2048,1792]{0,1:T(8,128)(2,1)} collective-permute-done((bf16[2048,1792]{0,1:T(8,128)(2,1)}, bf16[2048,1792]{0,1:T(8,128)(2,1)}, u32[]{:S(2)}, u32[]{:S(2)}) %collective-permute-start.8) | collective-permute-done | bytes 7340064 | tf_op jit(solution)/shard_map/ppermute | solution.py:21
  1039.4 473.2 %collective-permute-done.7 = bf16[2048,1792]{0,1:T(8,128)(2,1)} collective-permute-done((bf16[2048,1792]{0,1:T(8,128)(2,1)}, bf16[2048,1792]{0,1:T(8,128)(2,1)}, u32[]{:S(2)}, u32[]{:S(2)}) %collective-permute-start.7) | collective-permute-done | bytes 7340064 | tf_op jit(solution)/shard_map/ppermute | solution.py:21
  1520.7 19.9 fusion.14
  1540.6 9.9 copy.15
  1550.5 115.9 %collective-permute-done.4 = bf16[2048,1792]{0,1:T(8,128)(2,1)} collective-permute-done((bf16[2048,1792]{0,1:T(8,128)(2,1)}, bf16[2048,1792]{0,1:T(8,128)(2,1)}, u32[]{:S(2)}, u32[]{:S(2)}) %collective-permute-start.4) | collective-permute-done | bytes 7340064 | tf_op jit(solution)/shard_map/ppermute | solution.py:21
  1666.4 157.3 %collective-permute-done.3 = bf16[2048,1792]{0,1:T(8,128)(2,1)} collective-permute-done((bf16[2048,1792]{0,1:T(8,128)(2,1)}, bf16[2048,1792]{0,1:T(8,128)(2,1)}, u32[]{:S(2)}, u32[]{:S(2)}) %collective-permute-start.3) | collective-permute-done | bytes 7340064 | tf_op jit(solution)/shard_map/ppermute | solution.py:21
  1823.7 160.8 %collective-permute-done.2 = bf16[2048,1792]{0,1:T(8,128)(2,1)} collective-permute-done((bf16[2048,1792]{0,1:T(8,128)(2,1)}, bf16[2048,1792]{0,1:T(8,128)(2,1)}, u32[]{:S(2)}, u32[]{:S(2)}) %collective-permute-start.2) | collective-permute-done | bytes 7340064 | tf_op jit(solution)/shard_map/ppermute | solution.py:21
  1985.4 19.9 fusion.13
  2005.3 9.9 copy.14
  (46 shorter events, 44.7 us)
Async XLA Ops:
  7.2 23.6 %all-gather.15.cloned.1.call-start = ((), (), s32[]{:S(2)}) async-start(), calls=%async_computation.8 | async-start | bytes 1966080 | tf_op jit(solution)/shard_map/all_gather | solution.py:44
  7.9 135.3 %all-gather.7.cloned.1.call-start = ((), (), s32[]{:S(2)}) async-start(), calls=%async_computation.2 | async-start | bytes 8257536 | tf_op jit(solution)/shard_map/all_gather | solution.py:52
  8.6 247.5 %all-gather.9.cloned.1.call-start = ((), (), s32[]{:S(2)}) async-start(), calls=%async_computation.3 | async-start | bytes 8257536 | tf_op jit(solution)/shard_map/all_gather | solution.py:57
  9.4 293.9 %reduce-scatter.3.cloned.1.call-start = ((), (), s32[]{:S(2)}) async-start(), calls=%async_computation.4 | async-start | bytes 3932160 | tf_op jit(solution)/shard_map/reduce_scatter | solution.py:75
  30.7 112.5 %copy-start.1 = (bf16[1,384,2048]{2,1,0:T(8,128)(2,1)S(1)}, bf16[1,384,2048]{2,1,0:T(8,128)(2,1)}, u32[]{:S(2)}) copy-start(bf16[1,384,2048]{2,1,0:T(8,128)(2,1)} %all-gather.15.cloned.1.call-done) | copy-start | bytes 4718596
  265.6 78.8 %reduce-scatter.5.cloned.1.call-start = ((), (), s32[]{:S(2)}) async-start(), calls=%async_computation.6 | async-start | bytes 3932160 | tf_op jit(solution)/shard_map/reduce_scatter | solution.py:97
  265.7 7.3 copy-start.2
  265.7 7.3 copy-start.3
  271.5 1.5 copy-start.4
  273.0 30.2 %copy-start = (bf16[1,96,2048]{2,1,0:T(8,128)(2,1)S(1)}, bf16[1,96,2048]{2,1,0:T(8,128)(2,1)}, u32[]{:S(2)}) copy-start(bf16[1,96,2048]{2,1,0:T(8,128)(2,1)} %param.10) | copy-start | bytes 1179652
  282.3 85.0 %all-gather.11.cloned.1.call-start = ((), (), s32[]{:S(2)}) async-start(), calls=%async_computation.5 | async-start | bytes 1966080 | tf_op jit(solution)/shard_map/all_gather | solution.py:77
  305.2 81.9 %all-gather.13.cloned.1.call-start = ((), (), s32[]{:S(2)}) async-start(), calls=%async_computation.7 | async-start | bytes 1966080 | tf_op jit(solution)/shard_map/all_gather | solution.py:101
  407.6 315.0 %collective-permute-start.9 = (bf16[2048,1792]{0,1:T(8,128)(2,1)}, bf16[2048,1792]{0,1:T(8,128)(2,1)}, u32[]{:S(2)}, u32[]{:S(2)}) collective-permute-start(bf16[2048,1792]{0,1:T(8,128)(2,1)} %fusion.7), channel_id=1, source_target_pairs={{0,16},{4,20},{8,24},{12,28},{16,0},{20,4},{24,8},{28,12},{1,17},{... | collective-permute-start | bytes 22020104 | tf_op jit(solution)/shard_map/ppermute | solution.py:21
  407.9 629.4 %collective-permute-start.8 = (bf16[2048,1792]{0,1:T(8,128)(2,1)}, bf16[2048,1792]{0,1:T(8,128)(2,1)}, u32[]{:S(2)}, u32[]{:S(2)}) collective-permute-start(bf16[2048,1792]{0,1:T(8,128)(2,1)} %fusion.7), channel_id=1, source_target_pairs={{0,24},{4,28},{8,0},{12,4},{16,8},{20,12},{24,16},{28,20},{1,25},{... | collective-permute-start | bytes 22020104 | tf_op jit(solution)/shard_map/ppermute | solution.py:21
  410.0 1102.6 %collective-permute-start.7 = (bf16[2048,1792]{0,1:T(8,128)(2,1)}, bf16[2048,1792]{0,1:T(8,128)(2,1)}, u32[]{:S(2)}, u32[]{:S(2)}) collective-permute-start(bf16[2048,1792]{0,1:T(8,128)(2,1)} %fusion.7), channel_id=1, source_target_pairs={{0,8},{4,12},{8,16},{12,20},{16,24},{20,28},{24,0},{28,4},{1,9},{5... | collective-permute-start | bytes 22020104 | tf_op jit(solution)/shard_map/ppermute | solution.py:21
  410.0 1102.6 %collective-permute-start.6 = (bf16[2048,1792]{0,1:T(8,128)(2,1)}, bf16[2048,1792]{0,1:T(8,128)(2,1)}, u32[]{:S(2)}, u32[]{:S(2)}) collective-permute-start(bf16[2048,1792]{0,1:T(8,128)(2,1)} %fusion.7), channel_id=1, source_target_pairs={{0,28},{4,0},{8,4},{12,8},{16,12},{20,16},{24,20},{28,24},{1,29},{... | collective-permute-start | bytes 22020104 | tf_op jit(solution)/shard_map/ppermute | solution.py:21
  412.4 1101.1 %collective-permute-start.5 = (bf16[2048,1792]{0,1:T(8,128)(2,1)}, bf16[2048,1792]{0,1:T(8,128)(2,1)}, u32[]{:S(2)}, u32[]{:S(2)}) collective-permute-start(bf16[2048,1792]{0,1:T(8,128)(2,1)} %fusion.7), channel_id=1, source_target_pairs={{0,4},{4,8},{8,12},{12,16},{16,20},{20,24},{24,28},{28,0},{1,5},{5... | collective-permute-start | bytes 22020104 | tf_op jit(solution)/shard_map/ppermute | solution.py:21
  722.6 943.8 %collective-permute-start.4 = (bf16[2048,1792]{0,1:T(8,128)(2,1)}, bf16[2048,1792]{0,1:T(8,128)(2,1)}, u32[]{:S(2)}, u32[]{:S(2)}) collective-permute-start(bf16[2048,1792]{0,1:T(8,128)(2,1)} %fusion.8), channel_id=1, source_target_pairs={{0,16},{4,20},{8,24},{12,28},{16,0},{20,4},{24,8},{28,12},{1,17},{... | collective-permute-start | bytes 22020104 | tf_op jit(solution)/shard_map/ppermute | solution.py:21
  1037.2 786.5 %collective-permute-start.3 = (bf16[2048,1792]{0,1:T(8,128)(2,1)}, bf16[2048,1792]{0,1:T(8,128)(2,1)}, u32[]{:S(2)}, u32[]{:S(2)}) collective-permute-start(bf16[2048,1792]{0,1:T(8,128)(2,1)} %fusion.8), channel_id=1, source_target_pairs={{0,24},{4,28},{8,0},{12,4},{16,8},{20,12},{24,16},{28,20},{1,25},{... | collective-permute-start | bytes 22020104 | tf_op jit(solution)/shard_map/ppermute | solution.py:21
  1512.6 471.9 %collective-permute-start.2 = (bf16[2048,1792]{0,1:T(8,128)(2,1)}, bf16[2048,1792]{0,1:T(8,128)(2,1)}, u32[]{:S(2)}, u32[]{:S(2)}) collective-permute-start(bf16[2048,1792]{0,1:T(8,128)(2,1)} %fusion.8), channel_id=1, source_target_pairs={{0,8},{4,12},{8,16},{12,20},{16,24},{20,28},{24,0},{28,4},{1,9},{5... | collective-permute-start | bytes 22020104 | tf_op jit(solution)/shard_map/ppermute | solution.py:21
  1512.6 471.9 %collective-permute-start.1 = (bf16[2048,1792]{0,1:T(8,128)(2,1)}, bf16[2048,1792]{0,1:T(8,128)(2,1)}, u32[]{:S(2)}, u32[]{:S(2)}) collective-permute-start(bf16[2048,1792]{0,1:T(8,128)(2,1)} %fusion.8), channel_id=1, source_target_pairs={{0,28},{4,0},{8,4},{12,8},{16,12},{20,16},{24,20},{28,24},{1,29},{... | collective-permute-start | bytes 22020104 | tf_op jit(solution)/shard_map/ppermute | solution.py:21
  1513.5 471.9 %collective-permute-start = (bf16[2048,1792]{0,1:T(8,128)(2,1)}, bf16[2048,1792]{0,1:T(8,128)(2,1)}, u32[]{:S(2)}, u32[]{:S(2)}) collective-permute-start(bf16[2048,1792]{0,1:T(8,128)(2,1)} %fusion.8), channel_id=1, source_target_pairs={{0,4},{4,8},{8,12},{12,16},{16,20},{20,24},{24,28},{28,0},{1,5},{5... | collective-permute-start | bytes 22020104 | tf_op jit(solution)/shard_map/ppermute | solution.py:21
Sparse Core Ops, SparseCore 0:
  9.6 21.1 all-gather.14
  32.9 110.2 all-gather.6
  145.3 110.7 all-gather.8
  265.7 37.4 reduce-scatter.2
  306.4 37.9 reduce-scatter.4
  345.8 20.0 all-gather.10
  367.4 19.6 all-gather.12
where the time goes:
time: 2020 us
  waiting for transfers between devices  1810 us (90%)
  matrix products  84.8 us (4%)
  local copies, waits for them, and re-layouts  52.7 us (3%)
  other arithmetic  46.5 us (2%)
    ppermute x10, waiting for transfers between devices, passed_along(): return lax.ppermute(value, axis, pairs)  1500 us
    all_gather x1, waiting for transfers between devices, local(): down_full = lax.all_gather(down_weight, 'replica', axis=1, tiled=True)  105 us
    all_gather x1, waiting for transfers between devices, local(): lax.all_gather(up_weight, 'replica', axis=0, tiled=True)  104 us
    unnamed x15, local copies, waits for them, and re-layouts  52.7 us
  transfers between devices with their start and end apart: 17, of which 14 were waited for; matrix products, arithmetic and copies ran while one was open for 6% of the time, Pallas kernels for 0%

commit v1 on v0

v1 whole, which is shorter than its diff:
```python
import functools
import math

import jax
import jax.numpy as jnp
import numpy as np
from jax import lax
from jax.experimental import pallas as pl
from jax.experimental.pallas import tpu as pltpu
from jax.sharding import PartitionSpec as P

DEN = 64

step_size = 0.1
floor_value = 0.1
tracker_decay = 0.75

VMEM_BYTES = 40 * 1024 * 1024


def send(value, pairs):
    return lax.ppermute(value, "replica", pairs)


def step_body(inv_width, xt_ref, grad_ref, weight_ref, tracker_ref, out_ref):
    gradient = jnp.dot(xt_ref[...], grad_ref[...], preferred_element_type=jnp.float32) * inv_width
    ratio = gradient / jnp.maximum(tracker_ref[...].astype(jnp.float32), floor_value)
    out_ref[...] = (
        weight_ref[...].astype(jnp.float32) - step_size * jnp.clip(ratio, -1.0, 1.0)
    ).astype(out_ref.dtype)


def track_body(inv_width, xt_ref, grad_ref, probe_ref, tracker_ref, out_ref):
    curvature = jnp.dot(xt_ref[...], grad_ref[...], preferred_element_type=jnp.float32) * inv_width
    out_ref[...] = (
        tracker_decay * tracker_ref[...].astype(jnp.float32)
        + (1.0 - tracker_decay) * probe_ref[...].astype(jnp.float32) * curvature
    ).astype(out_ref.dtype)


def update_rows(body, name, tokens_t, grads, first, second):
    rows, width = first.shape
    depth = grads.shape[0]
    size = min(rows, 256)
    row_spec = pl.BlockSpec((size, width), lambda i: (i, 0))
    return pl.pallas_call(
        functools.partial(body, 1.0 / math.sqrt(rows)),
        grid=(rows // size,),
        in_specs=[
            pl.BlockSpec((size, depth), lambda i: (i, 0)),
            pl.BlockSpec((depth, width), lambda i: (0, 0)),
            row_spec,
            row_spec,
        ],
        out_specs=row_spec,
        out_shape=jax.ShapeDtypeStruct((rows, width), jnp.bfloat16),
        compiler_params=pltpu.CompilerParams(vmem_limit_bytes=VMEM_BYTES),
        name=name,
    )(tokens_t, grads, first, second)


def weighted_body(count, scale_ref, *refs):
    total = scale_ref[0] * refs[0][...].astype(jnp.float32)
    for k in range(1, count):
        total = total + scale_ref[k] * refs[k][...].astype(jnp.float32)
    refs[-1][...] = total.astype(refs[-1].dtype)


def weighted_sum(name, scales, parts):
    rows, width = parts[0].shape
    size = min(rows, 128)
    row_spec = pl.BlockSpec((size, width), lambda i: (i, 0))
    return pl.pallas_call(
        functools.partial(weighted_body, len(parts)),
        grid=(rows // size,),
        in_specs=[pl.BlockSpec(memory_space=pltpu.SMEM)] + [row_spec] * len(parts),
        out_specs=row_spec,
        out_shape=jax.ShapeDtypeStruct((rows, width), jnp.bfloat16),
        compiler_params=pltpu.CompilerParams(vmem_limit_bytes=VMEM_BYTES),
        name=name,
    )(scales, *parts)


def after(value, *earlier):
    def body(value_ref, *refs):
        refs[-1][...] = value_ref[...]

    return pl.pallas_call(
        body,
        in_specs=[pl.BlockSpec(memory_space=pltpu.VMEM)]
        + [pl.BlockSpec(memory_space=pl.ANY)] * len(earlier),
        out_specs=pl.BlockSpec(memory_space=pltpu.VMEM),
        out_shape=jax.ShapeDtypeStruct(value.shape, value.dtype),
        compiler_params=pltpu.CompilerParams(vmem_limit_bytes=VMEM_BYTES),
        name="after",
    )(value, *earlier)


def blank(shape, dtype):
    def body(out_ref):
        pass

    return pl.pallas_call(
        body,
        out_specs=pl.BlockSpec(memory_space=pl.ANY),
        out_shape=jax.ShapeDtypeStruct(shape, dtype),
        name="blank",
    )()


def by_rows(body, name, results, *operands):
    rows, width = operands[0].shape
    size = rows // 4 if rows % 64 == 0 else rows
    row_spec = pl.BlockSpec((size, width), lambda i: (i, 0))
    return pl.pallas_call(
        body,
        grid=(rows // size,),
        in_specs=[row_spec] * len(operands),
        out_specs=[row_spec] * len(results),
        out_shape=[jax.ShapeDtypeStruct((rows, width), kind) for kind in results],
        compiler_params=pltpu.CompilerParams(vmem_limit_bytes=VMEM_BYTES),
        name=name,
    )(*operands)


def chip_sum_body(mine_ref, theirs_ref, sum_ref, sent_ref):
    total = mine_ref[...] + theirs_ref[...]
    sum_ref[...] = total
    sent_ref[...] = total.astype(sent_ref.dtype)


def residual_body(chip_ref, beyond_ref, target_ref, out_ref):
    total = chip_ref[...] + beyond_ref[...].astype(jnp.float32)
    out_ref[...] = (total - target_ref[...].astype(jnp.float32)).astype(out_ref.dtype)


def tangent_body(chip_ref, beyond_ref, out_ref):
    total = chip_ref[...] + beyond_ref[...].astype(jnp.float32)
    out_ref[...] = total.astype(out_ref.dtype)


def turned(value):
    rows, width = value.shape
    size = 256

    def body(value_ref, out_ref):
        out_ref[...] = value_ref[...].T

    return pl.pallas_call(
        body,
        grid=(width // size,),
        in_specs=[pl.BlockSpec((rows, size), lambda i: (0, i))],
        out_specs=pl.BlockSpec((size, rows), lambda i: (i, 0)),
        out_shape=jax.ShapeDtypeStruct((width, rows), value.dtype),
        compiler_params=pltpu.CompilerParams(vmem_limit_bytes=VMEM_BYTES),
        name="turned",
    )(value)


def half_rows(*arrays):
    beyond = lax.ppermute(
        jnp.concatenate(arrays, axis=0), "tensor", [(0, 2), (2, 0), (1, 3), (3, 1)]
    )
    first = lax.axis_index("tensor") < 2
    found = []
    for rows, other in zip(arrays, jnp.split(beyond, len(arrays), axis=0)):
        found.append(
            jnp.concatenate([jnp.where(first, rows, other), jnp.where(first, other, rows)], axis=0)
        )
    return found


def other_core(value):
    return lax.ppermute(value, "tensor", [(0, 1), (1, 0), (2, 3), (3, 2)])


def both_halves(half):
    return jnp.concatenate([half, other_core(half)], axis=0)


class Swaps:
    def inputs(self, tokens, targets):
        half, target_half = half_rows(tokens, targets)
        return both_halves(half), target_half

    def residual(self, term, source, targets=None):
        half = source.shape[0] // 2
        theirs = other_core(term(source[half:]))
        chip, sent = by_rows(
            chip_sum_body, "chip_sum", (jnp.float32, jnp.bfloat16), term(source[:half]), theirs
        )
        beyond = lax.ppermute(sent, "tensor", [(0, 2), (2, 0), (1, 3), (3, 1)])
        if targets is None:
            (piece,) = by_rows(tangent_body, "tangent_res", (jnp.bfloat16,), chip, beyond)
        else:
            (piece,) = by_rows(residual_body, "residual", (jnp.bfloat16,), chip, beyond, targets)
        return both_halves(piece)


class Gathers:
    def whole(self, rows):
        return lax.all_gather(rows, "tensor", axis=0, tiled=True)

    def inputs(self, tokens, targets):
        return self.whole(tokens), targets

    def residual(self, term, source, targets=None):
        total = lax.psum_scatter(term(source), "tensor", scatter_dimension=0, tiled=True)
        if targets is not None:
            total = total - targets.astype(jnp.float32)
        return self.whole(total.astype(jnp.bfloat16))


def ring_order(count):
    if count == 8:
        return [0, 2, 4, 6, 7, 5, 3, 1]
    return list(range(count))


def ring_gather(block, axis):
    count = lax.axis_size("replica")
    order = ring_order(count)
    onward = [(order[i], order[(i + 1) % count]) for i in range(count)]
    back = [(b, a) for a, b in onward]
    place = [0] * count
    for at, replica in enumerate(order):
        place[replica] = at
    here = jnp.array(place, jnp.int32)[lax.axis_index("replica")]
    owner = jnp.array(order, jnp.int32)
    extent = block.shape[axis]
    shape = list(block.shape)
    shape[axis] = extent * count
    whole = blank(tuple(shape), block.dtype)

    def put(whole, piece, step, start=0):
        at = owner[jnp.mod(here + step, count)] * extent + start
        index = [0] * block.ndim
        index[axis] = at
        return lax.dynamic_update_slice(whole, piece, index)

    whole = put(whole, block, 0)
    ahead = behind = block
    full_steps = (count - 1) // 2
    near_end = block
    for step in range(1, full_steps + 1):
        ahead = send(ahead, onward)
        behind = send(behind, back)
        if step == full_steps - 1:
            near_end = ahead
        whole = put(whole, ahead, -step)
        whole = put(whole, behind, step)
    if count % 2 == 0:
        half = extent // 2
        first = lax.slice_in_dim(ahead, 0, half, axis=axis)
        second = lax.slice_in_dim(behind, half, extent, axis=axis)
        whole = put(whole, send(first, onward), -(full_steps + 1))
        whole = put(whole, send(second, back), full_steps + 1, half)
    return whole, near_end


def link_matrix(neighbours, numerators):
    count = neighbours.shape[0]
    ids = jnp.arange(count, dtype=neighbours.dtype)
    listed = jnp.sum(
        jnp.where(neighbours[:, :, None] == ids[None, None, :], numerators[:, :, None], 0), axis=1
    )
    own = DEN - jnp.sum(numerators, axis=1)
    return (listed + jnp.diag(own)).astype(jnp.float32) / DEN


class Grid:
    outer = [(2 * a + x, 2 * b + x) for a, b in ((0, 1), (1, 0), (2, 3), (3, 2)) for x in (0, 1)]
    inner = [(2 * a + x, 2 * b + x) for a, b in ((1, 2), (2, 1)) for x in (0, 1)]
    across = [(2 * z + x, 2 * z + 1 - x) for z in range(4) for x in (0, 1)]

    @staticmethod
    def picks():
        found = np.zeros((8, 10, 8, 8), np.float32)
        for r in range(8):
            z, x = divmod(r, 2)
            inside = z in (1, 2)
            swapped = 2 * (z ^ 1) + x
            middle = 2 * (3 - z) + x
            far = (6 if z == 1 else 0) + x
            other = 2 * z + 1 - x
            edge = (0 if z == 1 else 6) + x
            found[r, 0, r, r] = found[r, 1, r, swapped] = 1
            found[r, 4, other, r] = found[r, 5, other, swapped] = 1
            if inside:
                found[r, 2, r, middle] = found[r, 3, r, far] = 1
                found[r, 6, other, middle] = 1
                found[r, 7, edge, middle] = found[r, 8, edge, far] = 1
        found[2, 9, 0, 7] = found[5, 9, 7, 0] = 1
        return found


LAG = 2
STEPS = 2


def tick_kernel(plan, inv_width, *refs):
    names, results = plan
    got = dict(zip(names + results, refs))
    scale_ref = got["scales"]

    def weighted(first, *parts):
        total = None
        for k, part in enumerate(parts):
            term = scale_ref[first + k] * got[part][...].astype(jnp.float32)
            total = term if total is None else total + term
        return total

    put = {}
    if "grads" in got:
        slope = (
            jnp.dot(got["tokens_t"][...], got["grads"][...], preferred_element_type=jnp.float32)
            * inv_width
        )
        base = got["base"][...].astype(jnp.float32)
        tracked = got["tracker"][...].astype(jnp.float32)
        if "step" in names:
            ratio = slope / jnp.maximum(tracked, floor_value)
            made = base - step_size * jnp.clip(ratio, -1.0, 1.0)
        else:
            made = tracker_decay * tracked + (1.0 - tracker_decay) * base * slope
        put["made"] = made.astype(jnp.bfloat16)
    if "cross_own" in got:
        put["cross"] = weighted(4, "cross_own", "cross_swapped", "cross_middle").astype(jnp.bfloat16)
        put["pass_swapped"] = got["cross_swapped"][...]
    if "pass_far" in got:
        put["pass_far"] = got["pass_far"][...]
    if "out_middle" in got:
        put["outward"] = weighted(7, "out_middle", "out_far", "out_wrapped").astype(jnp.bfloat16)
    step = pl.program_id(0)
    for result in results:
        if result != "mixed":
            offset = 0
            for piece in result.split(":")[1].split("+"):
                rows = put[piece].shape[0]
                start = pl.multiple_of(offset + step * rows, rows)
                got[result][pl.ds(start, rows), :] = put[piece]
                offset += rows * STEPS
    if "mixed" in got:
        total = weighted(0, "own", "swapped", "middle", "far")
        total = total + got["sideways"][...].astype(jnp.float32)
        got["mixed"][...] = (total + got["rest"][...].astype(jnp.float32)).astype(jnp.bfloat16)


class Pipeline:
    def __init__(self, links, full_rows, width):
        me = lax.axis_index("replica")
        self.scales = jnp.sum(jnp.asarray(Grid.picks())[me] * links, axis=(1, 2))
        self.full_rows, self.width = full_rows, width
        self.place = {}
        self.last = None

    def parts(self, count):
        unit = self.full_rows // 64
        head, tail = [2, 2], [2, 2, 1, 1, 1, 1]
        found = []
        for which in range(count):
            ends = (head if which == 0 else []), (tail if which == count - 1 else [])
            middle = (64 - sum(ends[0]) - sum(ends[1])) // 4
            row = 0
            for size in ends[0] + [4] * middle + ends[1]:
                found.append((which, row, size * unit))
                row += size * unit
        return found

    def run(self, sources):
        parts = self.parts(len(sources))
        mixed = [None] * len(sources)
        for tick in range(len(parts) + 4 * LAG):
            self.tick(tick, parts, sources, mixed)
        return mixed

    def tick(self, tick, parts, sources, mixed):
        width = self.width
        count = len(parts)
        names, operands, specs = ["scales"], [self.scales], [pl.BlockSpec(memory_space=pltpu.SMEM)]
        place = self.place

        def row_spec(depth, start, rows):
            block = rows // STEPS
            return pl.BlockSpec((block, depth), lambda i: (start // block + i, 0))

        def add(name, key):
            array, start = place[key]
            names.append(name)
            operands.append(array)
            specs.append(row_spec(width, start, parts[key[1]][2]))

        payloads = {"outer": [], "inner": [], "across": []}
        flops = 0
        part = tick - 3 * LAG
        if 0 <= part < count:
            add("out_middle", ("middle", part))
            add("out_far", ("far", part))
            add("out_wrapped", ("wrapped", part))
            payloads["outer"].append(("outward", "rest", part))
        part = tick - 2 * LAG
        if 0 <= part < count:
            add("pass_far", ("far", part))
            payloads["across"].append(("pass_far", "wrapped", part))
        part = tick - LAG
        if 0 <= part < count:
            add("cross_own", ("own", part))
            add("cross_swapped", ("swapped", part))
            add("cross_middle", ("middle", part))
            payloads["inner"].append(("pass_swapped", "far", part))
            payloads["across"].append(("cross", "sideways", part))
        part = tick
        if part < count:
            which, start, rows = parts[part]
            tokens_t, grads, base, tracker, kind = sources[which]
            depth = grads.shape[0]
            names += ["tokens_t", "grads", "base", "tracker", kind]
            operands += [tokens_t, grads, base, tracker, self.scales]
            specs += [
                row_spec(depth, start, rows),
                pl.BlockSpec((depth, width), lambda i: (0, 0)),
                row_spec(width, start, rows),
                row_spec(width, start, rows),
                pl.BlockSpec(memory_space=pltpu.SMEM),
            ]
            payloads["outer"].append(("made", "swapped", part))
            payloads["inner"].append(("made", "middle", part))
            flops += 2 * rows * depth * width
        results, shapes, out_specs = [], [], []
        ways = [way for way, pieces in payloads.items() if pieces]
        moved = 0
        for way in ways:
            rows = sum(parts[piece[2]][2] for piece in payloads[way])
            moved += 2 * rows
            results.append(way + ":" + "+".join(piece[0] for piece in payloads[way]))
            shapes.append(jax.ShapeDtypeStruct((rows, width), jnp.bfloat16))
            out_specs.append(pl.BlockSpec((rows, width), lambda i: (0, 0)))
        aliases = {}
        part = tick - 4 * LAG
        if 0 <= part < count:
            for name in ("own", "swapped", "middle", "far", "sideways", "rest"):
                add(name, (name, part))
            which, start, rows = parts[part]
            if mixed[which] is not None:
                aliases = {len(operands): len(results)}
                names.append("target")
                operands.append(mixed[which])
                specs.append(pl.BlockSpec(memory_space=pl.ANY))
            moved += 7 * rows
            results.append("mixed")
            shapes.append(jax.ShapeDtypeStruct((self.full_rows, width), jnp.bfloat16))
            out_specs.append(row_spec(width, start, rows))
        if self.last is not None:
            names.append("earlier")
            operands.append(self.last)
            specs.append(pl.BlockSpec(memory_space=pl.ANY))
        got = pl.pallas_call(
            functools.partial(
                tick_kernel, (tuple(names), tuple(results)), 1.0 / math.sqrt(self.full_rows)
            ),
            grid=(STEPS,),
            in_specs=specs,
            out_specs=out_specs,
            out_shape=shapes,
            input_output_aliases=aliases,
            compiler_params=pltpu.CompilerParams(vmem_limit_bytes=VMEM_BYTES),
            cost_estimate=pl.CostEstimate(
                flops=flops, bytes_accessed=2 * moved * width, transcendentals=0
            ),
            name="tick",
        )(*operands)
        if results[-1] == "mixed":
            mixed[which] = got[-1]
        for way, payload in zip(ways, got):
            self.last = payload
            received = send(payload, getattr(Grid, way))
            start = 0
            for _, name, part in payloads[way]:
                place[name, part] = (received, start)
                if name == "swapped":
                    place["own", part] = (payload, start)
                start += parts[part][2]


class OffsetMixer:
    offsets = (1, -1, 2, -2, 4, -4)

    def __init__(self, links):
        count = lax.axis_size("replica")
        me = lax.axis_index("replica")
        self.steps = sorted({offset % count for offset in self.offsets})
        columns = jnp.stack([me] + [jnp.mod(me - step, count) for step in self.steps])
        self.scales = links[me][columns]
        self.pairs = [[(s, (s + step) % count) for s in range(count)] for step in self.steps]

    def mix(self, part):
        parts = [part] + [send(part, pairs) for pairs in self.pairs]
        return weighted_sum("mixed_rows", self.scales, parts)


def local(
    tokens, targets, gate_weight, probes, tracker, up_weight, down_weight, neighbours, numerators
):
    weight_now = gate_weight[0]
    tracker_now = tracker[0]
    probe_here = probes[0]
    width = weight_now.shape[0]
    hidden_units = down_weight.shape[0] * lax.axis_size("tensor")
    inv_width = 1.0 / math.sqrt(width)
    inv_hidden = 1.0 / math.sqrt(hidden_units)

    links = link_matrix(neighbours, numerators)

    group = Swaps() if lax.axis_size("tensor") == 4 else Gathers()
    gathered, target_rows = group.inputs(tokens[0], targets[0])
    gathered_t = turned(gathered)
    up_full, near_end = ring_gather(up_weight, 0)
    down_full, _ = ring_gather(after(down_weight, near_end), 1)

    gate_pre = jnp.dot(gathered, weight_now, preferred_element_type=jnp.float32) * inv_width
    probe_pre = jnp.dot(gathered, probe_here, preferred_element_type=jnp.float32) * inv_width
    up_pre = jnp.dot(gathered, up_full, preferred_element_type=jnp.float32) * inv_width
    logistic = jax.nn.sigmoid(gate_pre)
    activated = gate_pre * logistic
    slope_one = logistic * (1.0 + gate_pre * (1.0 - logistic))
    slope_two = logistic * (1.0 - logistic) * (2.0 + gate_pre * (1.0 - 2.0 * logistic))
    hidden = (activated * up_pre).astype(jnp.bfloat16)
    tangent_hidden = (slope_one * probe_pre * up_pre).astype(jnp.bfloat16)

    def forward_term(source):
        return jnp.dot(source, down_full, preferred_element_type=jnp.float32) * inv_hidden

    def backward_rows(piece):
        return (
            lax.dot_general(
                piece, down_full, (((1,), (1,)), ((), ())), preferred_element_type=jnp.float32
            )
            * inv_hidden
        )

    grad_hidden = backward_rows(group.residual(forward_term, hidden, target_rows))
    grad_gate = (grad_hidden * up_pre * slope_one).astype(jnp.bfloat16)

    tangent_grad = backward_rows(group.residual(forward_term, tangent_hidden))
    tangent_gate = (
        (tangent_grad * slope_one + grad_hidden * slope_two * probe_pre) * up_pre
    ).astype(jnp.bfloat16)

    stepping = (gathered_t, grad_gate, weight_now, tracker_now)
    tracking = (gathered_t, tangent_gate, probe_here, tracker_now)
    if lax.axis_size("replica") == 8:
        pipeline = Pipeline(links, width, weight_now.shape[1])
        mixed_weights, mixed_tracker = pipeline.run([(*stepping, "step"), (*tracking, "track")])
    else:
        mixer = OffsetMixer(links)
        mixed_weights = mixer.mix(update_rows(step_body, "stepped_rows", *stepping))
        mixed_tracker = mixer.mix(update_rows(track_body, "tracked_rows", *tracking))
    return (mixed_weights[None], mixed_tracker[None])


def solution(mesh):
    return jax.shard_map(
        local,
        mesh=mesh,
        in_specs=(
            P("replica", "tensor", None),
            P("replica", "tensor", None),
            P("replica", None, "tensor"),
            P("replica", None, "tensor"),
            P("replica", None, "tensor"),
            P("replica", "tensor"),
            P("tensor", "replica"),
            P(),
            P(),
        ),
        out_specs=(P("replica", None, "tensor"), P("replica", None, "tensor")),
        check_vma=False,
    )
```

time: 2020 us -> 940 us (0.47)
  the two profiles are of different devices: /device:TPU:17 before, /device:TPU:0 now
where the time goes in v1:
time: 940 us; the launch traced here: 930 us
  waiting for transfers between devices  361 us (38%)
  starting transfers between devices  249 us (26%)
  Pallas kernels  164 us (17%)
  local copies, waits for them, and re-layouts  82.9 us (9%)
  matrix products  47.2 us (5%)
  between operations  16.7 us (2%)
    ppermute x137, waiting for transfers between devices, send(): return lax.ppermute(value, 'replica', pairs)  325 us
    ppermute x137, starting transfers between devices, send(): return lax.ppermute(value, 'replica', pairs)  245 us
    pallas_call x45, Pallas kernels, tick(): pl.pallas_call(functools.partial(tick_kernel, (tuple(names), tuple(result...  157 us
    unnamed x420, local copies, waits for them, and re-layouts  70.9 us
    ppermute x2, waiting for transfers between devices, residual(): beyond = lax.ppermute(sent, 'tensor', [(0, 2), (2, 0), (1, 3), (3, 1)])  19.5 us
  transfers between devices with their start and end apart: 145, of which 51 were waited for; matrix products, arithmetic and copies ran while one was open for 6% of the time, Pallas kernels for 17%

profile of v1, /device:TPU:0, one launch (start us, length us, event | category | flops | bytes accessed | tf_op | source)
XLA Modules:
  0.0 929.7 jit_solution(8678143669098234495)
XLA Ops:
  6.9 15.5 %collective-permute-done = bf16[192,2048]{1,0:T(8,128)(2,1)S(1)} collective-permute-done((bf16[192,2048]{1,0:T(8,128)(2,1)S(1)}, bf16[192,2048]{1,0:T(8,128)(2,1)S(1)}, u32[]{:S(2)}, u32[]{:S(2)}) %collective-permute-start) | collective-permute-done | bytes 786464 | tf_op jit(solution)/shard_map/ppermute | solution.py:161
  63.9 30.6 %collective-permute-done.6 = bf16[256,1792]{1,0:T(8,128)(2,1)S(1)} collective-permute-done((bf16[256,1792]{1,0:T(8,128)(2,1)}, bf16[256,1792]{1,0:T(8,128)(2,1)S(1)}, u32[]{:S(2)}, u32[]{:S(2)}) %collective-permute-start.6) | collective-permute-done | bytes 917536 | tf_op jit(solution)/shard_map/ppermute | solution.py:22
  109.8 16.7 %collective-permute-done.12 = bf16[1792,256]{1,0:T(8,128)(2,1)S(1)} collective-permute-done((bf16[1792,256]{1,0:T(8,128)(2,1)S(1)}, bf16[1792,256]{1,0:T(8,128)(2,1)S(1)}, u32[]{:S(2)}, u32[]{:S(2)}) %collective-permute-start.12) | collective-permute-done | bytes 917536 | tf_op jit(solution)/shard_map/ppermute | solution.py:22
  134.6 12.9 %collective-permute-done.14 = bf16[1792,256]{1,0:T(8,128)(2,1)S(1)} collective-permute-done((bf16[1792,256]{1,0:T(8,128)(2,1)S(1)}, bf16[1792,256]{1,0:T(8,128)(2,1)S(1)}, u32[]{:S(2)}, u32[]{:S(2)}) %collective-permute-start.14) | collective-permute-done | bytes 917536 | tf_op jit(solution)/shard_map/ppermute | solution.py:22
  167.7 17.0 %collective-permute-done.19.beyond_ref = bf16[192,2048]{1,0:T(8,128)(2,1)S(1)} collective-permute-done((bf16[192,2048]{1,0:T(8,128)(2,1)S(1)}, bf16[192,2048]{1,0:T(8,128)(2,1)S(1)}, u32[]{:S(2)}, u32[]{:S(2)}) %collective-permute-start.19) | collective-permute-done | bytes 786464 | tf_op jit(solution)/shard_map/ppermute | solution.py:192
  221.4 13.9 %collective-permute-done.25.refs_2_.refs_14_ = bf16[64,1792]{1,0:T(8,128)(2,1)S(1)} collective-permute-done((bf16[64,1792]{1,0:T(8,128)(2,1)S(1)}, bf16[64,1792]{1,0:T(8,128)(2,1)S(1)}, u32[]{:S(2)}, u32[]{:S(2)}) %collective-permute-start.25) | collective-permute-done | bytes 229408 | tf_op jit(solution)/shard_map/ppermute | solution.py:22
  241.5 10.8 %collective-permute-start.31 = (bf16[128,1792]{1,0:T(8,128)(2,1)S(1)}, bf16[128,1792]{1,0:T(8,128)(2,1)S(1)}, u32[]{:S(2)}, u32[]{:S(2)}) collective-permute-start(bf16[128,1792]{1,0:T(8,128)(2,1)S(1)} %get-tuple-element.176.refs_2_.refs_13_), channel_id=1, source_target_pairs={{0,8},{4,12},{8,0},{12,4},{16,24},{20,28},{24,16},{28,20},{1,9},{5... | collective-permute-start | bytes 1376264 | tf_op jit(solution)/shard_map/ppermute | solution.py:22
  252.7 11.0 %collective-permute-done.31.refs_3_.refs_14_ = bf16[128,1792]{1,0:T(8,128)(2,1)S(1)} collective-permute-done((bf16[128,1792]{1,0:T(8,128)(2,1)S(1)}, bf16[128,1792]{1,0:T(8,128)(2,1)S(1)}, u32[]{:S(2)}, u32[]{:S(2)}) %collective-permute-start.31) | collective-permute-done | bytes 458784 | tf_op jit(solution)/shard_map/ppermute | solution.py:22
  275.4 11.0 %collective-permute-start.34 = (bf16[192,1792]{1,0:T(8,128)(2,1)S(1)}, bf16[192,1792]{1,0:T(8,128)(2,1)S(1)}, u32[]{:S(2)}, u32[]{:S(2)}) collective-permute-start(bf16[192,1792]{1,0:T(8,128)(2,1)S(1)} %get-tuple-element.180.refs_5_.refs_13_), channel_id=1, source_target_pairs={{0,8},{4,12},{8,0},{12,4},{16,24},{20,28},{24,16},{28,20},{1,9},{5... | collective-permute-start | bytes 2064392 | tf_op jit(solution)/shard_map/ppermute | solution.py:22
  291.6 14.4 %collective-permute-start.44 = (bf16[192,1792]{1,0:T(8,128)(2,1)S(1)}, bf16[192,1792]{1,0:T(8,128)(2,1)S(1)}, u32[]{:S(2)}, u32[]{:S(2)}) collective-permute-start(bf16[192,1792]{1,0:T(8,128)(2,1)S(1)} %get-tuple-element.188.refs_5_.refs_13_), channel_id=1, source_target_pairs={{0,8},{4,12},{8,0},{12,4},{16,24},{20,28},{24,16},{28,20},{1,9},{5... | collective-permute-start | bytes 2064392 | tf_op jit(solution)/shard_map/ppermute | solution.py:22
  320.3 17.8 %collective-permute-done.45.refs_17_ = bf16[64,1792]{1,0:T(8,128)(2,1)S(1)} collective-permute-done((bf16[64,1792]{1,0:T(8,128)(2,1)}, bf16[64,1792]{1,0:T(8,128)(2,1)S(1)}, u32[]{:S(2)}, u32[]{:S(2)}) %collective-permute-start.45) | collective-permute-done | bytes 229408 | tf_op jit(solution)/shard_map/ppermute | solution.py:22
  346.8 15.8 %collective-permute-start.51 = (bf16[256,1792]{1,0:T(8,128)(2,1)S(1)}, bf16[256,1792]{1,0:T(8,128)(2,1)S(1)}, u32[]{:S(2)}, u32[]{:S(2)}) collective-permute-start(bf16[256,1792]{1,0:T(8,128)(2,1)S(1)} %get-tuple-element.196.refs_5_.refs_13_), channel_id=1, source_target_pairs={{0,8},{4,12},{8,0},{12,4},{16,24},{20,28},{24,16},{28,20},{1,9},{5... | collective-permute-start | bytes 2752520 | tf_op jit(solution)/shard_map/ppermute | solution.py:22
  368.5 12.1 %collective-permute-done.49.refs_3_.refs_17_ = bf16[256,1792]{1,0:T(8,128)(2,1)S(1)} collective-permute-done((bf16[256,1792]{1,0:T(8,128)(2,1)S(1)}, bf16[256,1792]{1,0:T(8,128)(2,1)S(1)}, u32[]{:S(2)}, u32[]{:S(2)}) %collective-permute-start.49) | collective-permute-done | bytes 917536 | tf_op jit(solution)/shard_map/ppermute | solution.py:22
  407.4 9.6 %collective-permute-done.55.refs_3_.refs_17_ = bf16[256,1792]{1,0:T(8,128)(2,1)S(1)} collective-permute-done((bf16[256,1792]{1,0:T(8,128)(2,1)}, bf16[256,1792]{1,0:T(8,128)(2,1)S(1)}, u32[]{:S(2)}, u32[]{:S(2)}) %collective-permute-start.55) | collective-permute-done | bytes 917536 | tf_op jit(solution)/shard_map/ppermute | solution.py:22
  494.6 11.0 %fusion.3.refs_9_ = bf16[384,1792]{1,0:T(8,128)(2,1)S(1)} fusion(f32[384,1792]{1,0:T(8,128)} %get-tuple-element.340, bf16[1792,2048]{1,0:T(8,128)(2,1)} %copy-done.186, f32[384,1792]{1,0:T(8,128)} %get-tuple-element.341, f32[384,1792]{1,0:T(8,128)} %convolution_multiply_fusion.2, f32[384,1792]{1,0:T(8,128)} %copy-done.198, ...), kind=kOutput, calls=%fused_computation.10 | convolution fusion | flops 2835480576 | bytes 21299200 | tf_op jit(solution)/shard_map/dot_general | solution.py:535
  519.8 10.3 %collective-permute-done.66.refs_6_.refs_18_.refs_14_ = bf16[256,1792]{1,0:T(8,128)(2,1)S(1)} collective-permute-done((bf16[256,1792]{1,0:T(8,128)(2,1)}, bf16[256,1792]{1,0:T(8,128)(2,1)S(1)}, u32[]{:S(2)}, u32[]{:S(2)}) %collective-permute-start.66) | collective-permute-done | bytes 917536 | tf_op jit(solution)/shard_map/ppermute | solution.py:22
  557.2 13.2 %collective-permute-start.84 = (bf16[256,1792]{1,0:T(8,128)(2,1)}, bf16[256,1792]{1,0:T(8,128)(2,1)S(1)}, u32[]{:S(2)}, u32[]{:S(2)}) collective-permute-start(bf16[256,1792]{1,0:T(8,128)(2,1)} %get-tuple-element.238.refs_5_.refs_13_), channel_id=1, source_target_pairs={{0,8},{4,12},{8,0},{12,4},{16,24},{20,28},{24,16},{28,20},{1,9},{5... | collective-permute-start | bytes 2752520 | tf_op jit(solution)/shard_map/ppermute | solution.py:22
  580.6 11.2 %collective-permute-done.84.refs_6_.refs_18_.refs_14_ = bf16[256,1792]{1,0:T(8,128)(2,1)S(1)} collective-permute-done((bf16[256,1792]{1,0:T(8,128)(2,1)}, bf16[256,1792]{1,0:T(8,128)(2,1)S(1)}, u32[]{:S(2)}, u32[]{:S(2)}) %collective-permute-start.84) | collective-permute-done | bytes 917536 | tf_op jit(solution)/shard_map/ppermute | solution.py:22
  598.9 10.7 %collective-permute-start.90 = (bf16[256,1792]{1,0:T(8,128)(2,1)}, bf16[256,1792]{1,0:T(8,128)(2,1)S(1)}, u32[]{:S(2)}, u32[]{:S(2)}) collective-permute-start(bf16[256,1792]{1,0:T(8,128)(2,1)} %get-tuple-element.246.refs_5_.refs_13_), channel_id=1, source_target_pairs={{0,8},{4,12},{8,0},{12,4},{16,24},{20,28},{24,16},{28,20},{1,9},{5... | collective-permute-start | bytes 2752520 | tf_op jit(solution)/shard_map/ppermute | solution.py:22
  621.5 9.7 %collective-permute-done.90.refs_6_.refs_18_.refs_14_ = bf16[256,1792]{1,0:T(8,128)(2,1)S(1)} collective-permute-done((bf16[256,1792]{1,0:T(8,128)(2,1)}, bf16[256,1792]{1,0:T(8,128)(2,1)S(1)}, u32[]{:S(2)}, u32[]{:S(2)}) %collective-permute-start.90) | collective-permute-done | bytes 917536 | tf_op jit(solution)/shard_map/ppermute | solution.py:22
  698.1 11.4 %collective-permute-done.102.refs_6_.refs_18_.refs_14_ = bf16[256,1792]{1,0:T(8,128)(2,1)S(1)} collective-permute-done((bf16[256,1792]{1,0:T(8,128)(2,1)S(1)}, bf16[256,1792]{1,0:T(8,128)(2,1)S(1)}, u32[]{:S(2)}, u32[]{:S(2)}) %collective-permute-start.102) | collective-permute-done | bytes 917536 | tf_op jit(solution)/shard_map/ppermute | solution.py:22
  716.6 11.0 %collective-permute-start.108 = (bf16[256,1792]{1,0:T(8,128)(2,1)S(1)}, bf16[256,1792]{1,0:T(8,128)(2,1)S(1)}, u32[]{:S(2)}, u32[]{:S(2)}) collective-permute-start(bf16[256,1792]{1,0:T(8,128)(2,1)S(1)} %get-tuple-element.270.refs_5_.refs_13_), channel_id=1, source_target_pairs={{0,8},{4,12},{8,0},{12,4},{16,24},{20,28},{24,16},{28,20},{1,9},{5... | collective-permute-start | bytes 2752520 | tf_op jit(solution)/shard_map/ppermute | solution.py:22
  821.0 9.9 %collective-permute-done.120.refs_6_.refs_18_ = bf16[192,1792]{1,0:T(8,128)(2,1)S(1)} collective-permute-done((bf16[192,1792]{1,0:T(8,128)(2,1)S(1)}, bf16[192,1792]{1,0:T(8,128)(2,1)S(1)}, u32[]{:S(2)}, u32[]{:S(2)}) %collective-permute-start.120) | collective-permute-done | bytes 688160 | tf_op jit(solution)/shard_map/ppermute | solution.py:22
  854.2 12.9 %collective-permute-done.126.refs_6_.refs_18_.refs_5_ = bf16[160,1792]{1,0:T(8,128)(2,1)S(1)} collective-permute-done((bf16[160,1792]{1,0:T(8,128)(2,1)S(1)}, bf16[160,1792]{1,0:T(8,128)(2,1)S(1)}, u32[]{:S(2)}, u32[]{:S(2)}) %collective-permute-start.126) | collective-permute-done | bytes 573472 | tf_op jit(solution)/shard_map/ppermute | solution.py:22
  (787 shorter events, 592.6 us)
Async XLA Ops:
  52.1 44.7 %collective-permute-start.10 = (bf16[1792,256]{1,0:T(8,128)(2,1)S(1)}, bf16[1792,256]{1,0:T(8,128)(2,1)S(1)}, u32[]{:S(2)}, u32[]{:S(2)}) collective-permute-start(bf16[1792,256]{1,0:T(8,128)(2,1)S(1)} %after.1), channel_id=1, source_target_pairs={{0,8},{8,16},{16,24},{24,28},{28,20},{20,12},{12,4},{4,0},{1,9},{9... | collective-permute-start | bytes 2752520 | tf_op jit(solution)/shard_map/ppermute | solution.py:22
  53.7 40.8 %collective-permute-start.6 = (bf16[256,1792]{1,0:T(8,128)(2,1)}, bf16[256,1792]{1,0:T(8,128)(2,1)S(1)}, u32[]{:S(2)}, u32[]{:S(2)}) collective-permute-start(bf16[256,1792]{1,0:T(8,128)(2,1)} %collective-permute-done.4.refs_0_), channel_id=1, source_target_pairs={{0,8},{8,16},{16,24},{24,28},{28,20},{20,12},{12,4},{4,0},{1,9},{9... | collective-permute-start | bytes 2752520 | tf_op jit(solution)/shard_map/ppermute | solution.py:22
  55.3 40.9 %collective-permute-start.7 = (bf16[256,1792]{1,0:T(8,128)(2,1)}, bf16[256,1792]{1,0:T(8,128)(2,1)S(1)}, u32[]{:S(2)}, u32[]{:S(2)}) collective-permute-start(bf16[256,1792]{1,0:T(8,128)(2,1)} %collective-permute-done.5), channel_id=1, source_target_pairs={{8,0},{16,8},{24,16},{28,24},{20,28},{12,20},{4,12},{0,4},{9,1},{1... | collective-permute-start | bytes 2752520 | tf_op jit(solution)/shard_map/ppermute | solution.py:22
  60.4 38.1 %collective-permute-start.11 = (bf16[1792,256]{1,0:T(8,128)(2,1)S(1)}, bf16[1792,256]{1,0:T(8,128)(2,1)S(1)}, u32[]{:S(2)}, u32[]{:S(2)}) collective-permute-start(bf16[1792,256]{1,0:T(8,128)(2,1)S(1)} %after.1), channel_id=1, source_target_pairs={{8,0},{16,8},{24,16},{28,24},{20,28},{12,20},{4,12},{0,4},{9,1},{1... | collective-permute-start | bytes 2752520 | tf_op jit(solution)/shard_map/ppermute | solution.py:22
  240.7 32.1 %collective-permute-start.28 = (bf16[256,1792]{1,0:T(8,128)(2,1)S(1)}, bf16[256,1792]{1,0:T(8,128)(2,1)S(1)}, u32[]{:S(2)}, u32[]{:S(2)}) collective-permute-start(bf16[256,1792]{1,0:T(8,128)(2,1)S(1)} %get-tuple-element.173), channel_id=1, source_target_pairs={{8,16},{12,20},{16,8},{20,12},{9,17},{13,21},{17,9},{21,13},{10,18... | collective-permute-start | bytes 2752520 | tf_op jit(solution)/shard_map/ppermute | solution.py:22
  275.4 37.6 %collective-permute-start.34 = (bf16[192,1792]{1,0:T(8,128)(2,1)S(1)}, bf16[192,1792]{1,0:T(8,128)(2,1)S(1)}, u32[]{:S(2)}, u32[]{:S(2)}) collective-permute-start(bf16[192,1792]{1,0:T(8,128)(2,1)S(1)} %get-tuple-element.180.refs_5_.refs_13_), channel_id=1, source_target_pairs={{0,8},{4,12},{8,0},{12,4},{16,24},{20,28},{24,16},{28,20},{1,9},{5... | collective-permute-start | bytes 2064392 | tf_op jit(solution)/shard_map/ppermute | solution.py:22
  291.6 46.8 %collective-permute-start.44 = (bf16[192,1792]{1,0:T(8,128)(2,1)S(1)}, bf16[192,1792]{1,0:T(8,128)(2,1)S(1)}, u32[]{:S(2)}, u32[]{:S(2)}) collective-permute-start(bf16[192,1792]{1,0:T(8,128)(2,1)S(1)} %get-tuple-element.188.refs_5_.refs_13_), channel_id=1, source_target_pairs={{0,8},{4,12},{8,0},{12,4},{16,24},{20,28},{24,16},{28,20},{1,9},{5... | collective-permute-start | bytes 2064392 | tf_op jit(solution)/shard_map/ppermute | solution.py:22
  344.4 36.3 %collective-permute-start.49 = (bf16[256,1792]{1,0:T(8,128)(2,1)S(1)}, bf16[256,1792]{1,0:T(8,128)(2,1)S(1)}, u32[]{:S(2)}, u32[]{:S(2)}) collective-permute-start(bf16[256,1792]{1,0:T(8,128)(2,1)S(1)} %get-tuple-element.191.refs_20_), channel_id=1, source_target_pairs={{0,4},{4,0},{8,12},{12,8},{16,20},{20,16},{24,28},{28,24},{1,5},{5... | collective-permute-start | bytes 2752520 | tf_op jit(solution)/shard_map/ppermute | solution.py:22
  346.1 41.7 %collective-permute-start.50 = (bf16[256,1792]{1,0:T(8,128)(2,1)}, bf16[256,1792]{1,0:T(8,128)(2,1)S(1)}, u32[]{:S(2)}, u32[]{:S(2)}) collective-permute-start(bf16[256,1792]{1,0:T(8,128)(2,1)} %get-tuple-element.195), channel_id=1, source_target_pairs={{8,16},{12,20},{16,8},{20,12},{9,17},{13,21},{17,9},{21,13},{10,18... | collective-permute-start | bytes 2752520 | tf_op jit(solution)/shard_map/ppermute | solution.py:22
  346.8 41.1 %collective-permute-start.51 = (bf16[256,1792]{1,0:T(8,128)(2,1)S(1)}, bf16[256,1792]{1,0:T(8,128)(2,1)S(1)}, u32[]{:S(2)}, u32[]{:S(2)}) collective-permute-start(bf16[256,1792]{1,0:T(8,128)(2,1)S(1)} %get-tuple-element.196.refs_5_.refs_13_), channel_id=1, source_target_pairs={{0,8},{4,12},{8,0},{12,4},{16,24},{20,28},{24,16},{28,20},{1,9},{5... | collective-permute-start | bytes 2752520 | tf_op jit(solution)/shard_map/ppermute | solution.py:22
  387.8 45.2 %collective-permute-start.67 = (f32[192,2048]{1,0:T(8,128)S(1)}, f32[192,2048]{1,0:T(8,128)}, u32[]{:S(2)}, u32[]{:S(2)}) collective-permute-start(f32[192,2048]{1,0:T(8,128)S(1)} %convolution_multiply_fusion.5), channel_id=1, source_target_pairs={{0,1},{1,0},{2,3},{3,2},{4,5},{5,4},{6,7},{7,6},{8,9},{9,8},{10,11... | collective-permute-start | bytes 4718600 | tf_op jit(solution)/shard_map/ppermute | solution.py:174
  406.2 32.1 %collective-permute-start.52 = (bf16[256,1792]{1,0:T(8,128)(2,1)}, bf16[256,1792]{1,0:T(8,128)(2,1)S(1)}, u32[]{:S(2)}, u32[]{:S(2)}) collective-permute-start(bf16[256,1792]{1,0:T(8,128)(2,1)} %get-tuple-element.200), channel_id=1, source_target_pairs={{8,16},{12,20},{16,8},{20,12},{9,17},{13,21},{17,9},{21,13},{10,18... | collective-permute-start | bytes 2752520 | tf_op jit(solution)/shard_map/ppermute | solution.py:22
  426.6 33.6 %collective-permute-start.61 = (bf16[256,1792]{1,0:T(8,128)(2,1)}, bf16[256,1792]{1,0:T(8,128)(2,1)S(1)}, u32[]{:S(2)}, u32[]{:S(2)}) collective-permute-start(bf16[256,1792]{1,0:T(8,128)(2,1)} %get-tuple-element.207.refs_20_), channel_id=1, source_target_pairs={{0,4},{4,0},{8,12},{12,8},{16,20},{20,16},{24,28},{28,24},{1,5},{5... | collective-permute-start | bytes 2752520 | tf_op jit(solution)/shard_map/ppermute | solution.py:22
  471.6 34.9 %collective-permute-start.70 = (bf16[256,1792]{1,0:T(8,128)(2,1)}, bf16[256,1792]{1,0:T(8,128)(2,1)}, u32[]{:S(2)}, u32[]{:S(2)}) collective-permute-start(bf16[256,1792]{1,0:T(8,128)(2,1)} %get-tuple-element.215.refs_20_), channel_id=1, source_target_pairs={{0,4},{4,0},{8,12},{12,8},{16,20},{20,16},{24,28},{28,24},{1,5},{5... | collective-permute-start | bytes 2752520 | tf_op jit(solution)/shard_map/ppermute | solution.py:22
  473.3 34.9 %collective-permute-start.71 = (bf16[256,1792]{1,0:T(8,128)(2,1)}, bf16[256,1792]{1,0:T(8,128)(2,1)S(1)}, u32[]{:S(2)}, u32[]{:S(2)}) collective-permute-start(bf16[256,1792]{1,0:T(8,128)(2,1)} %get-tuple-element.221), channel_id=1, source_target_pairs={{8,16},{12,20},{16,8},{20,12},{9,17},{13,21},{17,9},{21,13},{10,18... | collective-permute-start | bytes 2752520 | tf_op jit(solution)/shard_map/ppermute | solution.py:22
  535.5 34.8 %collective-permute-start.74 = (bf16[256,1792]{1,0:T(8,128)(2,1)}, bf16[256,1792]{1,0:T(8,128)(2,1)S(1)}, u32[]{:S(2)}, u32[]{:S(2)}) collective-permute-start(bf16[256,1792]{1,0:T(8,128)(2,1)} %get-tuple-element.227.refs_20_), channel_id=1, source_target_pairs={{0,4},{4,0},{8,12},{12,8},{16,20},{20,16},{24,28},{28,24},{1,5},{5... | collective-permute-start | bytes 2752520 | tf_op jit(solution)/shard_map/ppermute | solution.py:22
  557.2 34.6 %collective-permute-start.84 = (bf16[256,1792]{1,0:T(8,128)(2,1)}, bf16[256,1792]{1,0:T(8,128)(2,1)S(1)}, u32[]{:S(2)}, u32[]{:S(2)}) collective-permute-start(bf16[256,1792]{1,0:T(8,128)(2,1)} %get-tuple-element.238.refs_5_.refs_13_), channel_id=1, source_target_pairs={{0,8},{4,12},{8,0},{12,4},{16,24},{20,28},{24,16},{28,20},{1,9},{5... | collective-permute-start | bytes 2752520 | tf_op jit(solution)/shard_map/ppermute | solution.py:22
  575.7 33.9 %collective-permute-start.80 = (bf16[256,1792]{1,0:T(8,128)(2,1)}, bf16[256,1792]{1,0:T(8,128)(2,1)S(1)}, u32[]{:S(2)}, u32[]{:S(2)}) collective-permute-start(bf16[256,1792]{1,0:T(8,128)(2,1)} %get-tuple-element.235.refs_20_), channel_id=1, source_target_pairs={{0,4},{4,0},{8,12},{12,8},{16,20},{20,16},{24,28},{28,24},{1,5},{5... | collective-permute-start | bytes 2752520 | tf_op jit(solution)/shard_map/ppermute | solution.py:22
  598.9 32.2 %collective-permute-start.90 = (bf16[256,1792]{1,0:T(8,128)(2,1)}, bf16[256,1792]{1,0:T(8,128)(2,1)S(1)}, u32[]{:S(2)}, u32[]{:S(2)}) collective-permute-start(bf16[256,1792]{1,0:T(8,128)(2,1)} %get-tuple-element.246.refs_5_.refs_13_), channel_id=1, source_target_pairs={{0,8},{4,12},{8,0},{12,4},{16,24},{20,28},{24,16},{28,20},{1,9},{5... | collective-permute-start | bytes 2752520 | tf_op jit(solution)/shard_map/ppermute | solution.py:22
  696.0 31.6 %collective-permute-start.98 = (bf16[256,1792]{1,0:T(8,128)(2,1)}, bf16[256,1792]{1,0:T(8,128)(2,1)S(1)}, u32[]{:S(2)}, u32[]{:S(2)}) collective-permute-start(bf16[256,1792]{1,0:T(8,128)(2,1)} %get-tuple-element.259.refs_20_), channel_id=1, source_target_pairs={{0,4},{4,0},{8,12},{12,8},{16,20},{20,16},{24,28},{28,24},{1,5},{5... | collective-permute-start | bytes 2752520 | tf_op jit(solution)/shard_map/ppermute | solution.py:22
  696.9 31.7 %collective-permute-start.99 = (bf16[256,1792]{1,0:T(8,128)(2,1)S(1)}, bf16[256,1792]{1,0:T(8,128)(2,1)S(1)}, u32[]{:S(2)}, u32[]{:S(2)}) collective-permute-start(bf16[256,1792]{1,0:T(8,128)(2,1)S(1)} %get-tuple-element.260.refs_5_.refs_13_), channel_id=1, source_target_pairs={{0,8},{4,12},{8,0},{12,4},{16,24},{20,28},{24,16},{28,20},{1,9},{5... | collective-permute-start | bytes 2752520 | tf_op jit(solution)/shard_map/ppermute | solution.py:22
  716.6 32.2 %collective-permute-start.108 = (bf16[256,1792]{1,0:T(8,128)(2,1)S(1)}, bf16[256,1792]{1,0:T(8,128)(2,1)S(1)}, u32[]{:S(2)}, u32[]{:S(2)}) collective-permute-start(bf16[256,1792]{1,0:T(8,128)(2,1)S(1)} %get-tuple-element.270.refs_5_.refs_13_), channel_id=1, source_target_pairs={{0,8},{4,12},{8,0},{12,4},{16,24},{20,28},{24,16},{28,20},{1,9},{5... | collective-permute-start | bytes 2752520 | tf_op jit(solution)/shard_map/ppermute | solution.py:22
  795.4 35.5 %collective-permute-start.118 = (bf16[256,1792]{1,0:T(8,128)(2,1)}, bf16[256,1792]{1,0:T(8,128)(2,1)S(1)}, u32[]{:S(2)}, u32[]{:S(2)}) collective-permute-start(bf16[256,1792]{1,0:T(8,128)(2,1)} %get-tuple-element.281.refs_20_), channel_id=1, source_target_pairs={{0,4},{4,0},{8,12},{12,8},{16,20},{20,16},{24,28},{28,24},{1,5},{5... | collective-permute-start | bytes 2752520 | tf_op jit(solution)/shard_map/ppermute | solution.py:22
  808.9 33.5 %collective-permute-start.116 = (bf16[256,1792]{1,0:T(8,128)(2,1)}, bf16[256,1792]{1,0:T(8,128)(2,1)S(1)}, u32[]{:S(2)}, u32[]{:S(2)}) collective-permute-start(bf16[256,1792]{1,0:T(8,128)(2,1)} %get-tuple-element.283.refs_20_), channel_id=1, source_target_pairs={{0,4},{4,0},{8,12},{12,8},{16,20},{20,16},{24,28},{28,24},{1,5},{5... | collective-permute-start | bytes 2752520 | tf_op jit(solution)/shard_map/ppermute | solution.py:22
  (330 other events, 4919.9 us)

commit v2 on v1

--- a/solution.py
+++ b/solution.py
@@ -15,7 +15,8 @@
 floor_value = 0.1
 tracker_decay = 0.75
 
-VMEM_BYTES = 40 * 1024 * 1024
+VMEM_BYTES = 16 * 1024 * 1024
+TICK_VMEM_BYTES = 40 * 1024 * 1024
 
 
 def send(value, pairs):
@@ -108,19 +109,24 @@
     )()
 
 
-def by_rows(body, name, results, *operands):
+def by_rows(body, name, results, *operands, earlier=()):
+    count = len(operands)
+
+    def without_earlier(*refs):
+        body(*refs[:count], *refs[count + len(earlier) :])
+
     rows, width = operands[0].shape
     size = rows // 4 if rows % 64 == 0 else rows
     row_spec = pl.BlockSpec((size, width), lambda i: (i, 0))
     return pl.pallas_call(
-        body,
+        without_earlier,
         grid=(rows // size,),
-        in_specs=[row_spec] * len(operands),
+        in_specs=[row_spec] * count + [pl.BlockSpec(memory_space=pl.ANY)] * len(earlier),
         out_specs=[row_spec] * len(results),
         out_shape=[jax.ShapeDtypeStruct((rows, width), kind) for kind in results],
         compiler_params=pltpu.CompilerParams(vmem_limit_bytes=VMEM_BYTES),
         name=name,
-    )(*operands)
+    )(*operands, *earlier)
 
 
 def chip_sum_body(mine_ref, theirs_ref, sum_ref, sent_ref):
@@ -137,6 +143,55 @@
 def tangent_body(chip_ref, beyond_ref, out_ref):
     total = chip_ref[...] + beyond_ref[...].astype(jnp.float32)
     out_ref[...] = total.astype(out_ref.dtype)
+
+
+def backward_product(inv_hidden, res_ref, down_ref):
+    return (
+        lax.dot_general(
+            res_ref[...],
+            down_ref[...],
+            (((1,), (1,)), ((), ())),
+            preferred_element_type=jnp.float32,
+        )
+        * inv_hidden
+    )
+
+
+def gate_body(inv_hidden, res_ref, down_ref, factor_ref, hidden_ref, gate_ref):
+    grad = backward_product(inv_hidden, res_ref, down_ref)
+    hidden_ref[...] = grad
+    gate_ref[...] = (grad * factor_ref[...]).astype(gate_ref.dtype)
+
+
+def tangent_gate_body(inv_hidden, res_ref, down_ref, factor_ref, hidden_ref, curve_ref, gate_ref):
+    grad = backward_product(inv_hidden, res_ref, down_ref)
+    gate = grad * factor_ref[...] + hidden_ref[...] * curve_ref[...]
+    gate_ref[...] = gate.astype(gate_ref.dtype)
+
+
+def backward(body, name, inv_hidden, kinds, res, down, *factors):
+    rows, width = res.shape
+    units = down.shape[0]
+    size = 256 if units % 256 == 0 else units
+    unit_spec = pl.BlockSpec((rows, size), lambda i: (0, i))
+    return pl.pallas_call(
+        functools.partial(body, inv_hidden),
+        grid=(units // size,),
+        in_specs=[
+            pl.BlockSpec((rows, width), lambda i: (0, 0)),
+            pl.BlockSpec((size, width), lambda i: (i, 0)),
+        ]
+        + [unit_spec] * len(factors),
+        out_specs=[unit_spec] * len(kinds),
+        out_shape=[jax.ShapeDtypeStruct((rows, units), kind) for kind in kinds],
+        compiler_params=pltpu.CompilerParams(vmem_limit_bytes=VMEM_BYTES),
+        cost_estimate=pl.CostEstimate(
+            flops=2 * rows * width * units,
+            bytes_accessed=2 * units * width + 10 * rows * units,
+            transcendentals=0,
+        ),
+        name=name,
+    )(res, down, *factors)
 
 
 def turned(value):
@@ -157,17 +212,12 @@
     )(value)
 
 
-def half_rows(*arrays):
-    beyond = lax.ppermute(
-        jnp.concatenate(arrays, axis=0), "tensor", [(0, 2), (2, 0), (1, 3), (3, 1)]
+def half_rows(rows):
+    beyond = lax.ppermute(rows, "tensor", [(0, 2), (2, 0), (1, 3), (3, 1)])
+    first = lax.axis_index("tensor") < 2
+    return jnp.concatenate(
+        [jnp.where(first, rows, beyond), jnp.where(first, beyond, rows)], axis=0
     )
-    first = lax.axis_index("tensor") < 2
-    found = []
-    for rows, other in zip(arrays, jnp.split(beyond, len(arrays), axis=0)):
-        found.append(
-            jnp.concatenate([jnp.where(first, rows, other), jnp.where(first, other, rows)], axis=0)
-        )
-    return found
 
 
 def other_core(value):
@@ -180,21 +230,34 @@
 
 class Swaps:
     def inputs(self, tokens, targets):
-        half, target_half = half_rows(tokens, targets)
-        return both_halves(half), target_half
-
-    def residual(self, term, source, targets=None):
+        return both_halves(half_rows(tokens)), half_rows(targets)
+
+    def terms(self, term, source):
         half = source.shape[0] // 2
         theirs = other_core(term(source[half:]))
+        return term(source[:half]), theirs
+
+    def sums(self, terms, earlier=()):
         chip, sent = by_rows(
-            chip_sum_body, "chip_sum", (jnp.float32, jnp.bfloat16), term(source[:half]), theirs
+            chip_sum_body, "chip_sum", (jnp.float32, jnp.bfloat16), *terms, earlier=earlier
         )
-        beyond = lax.ppermute(sent, "tensor", [(0, 2), (2, 0), (1, 3), (3, 1)])
-        if targets is None:
-            (piece,) = by_rows(tangent_body, "tangent_res", (jnp.bfloat16,), chip, beyond)
-        else:
-            (piece,) = by_rows(residual_body, "residual", (jnp.bfloat16,), chip, beyond, targets)
-        return both_halves(piece)
+        return chip, lax.ppermute(sent, "tensor", [(0, 2), (2, 0), (1, 3), (3, 1)])
+
+    def residuals(self, term, hidden, tangent_hidden, targets, earlier):
+        sums = self.sums(self.terms(term, hidden), earlier)
+        tangent_terms = self.terms(term, tangent_hidden)
+        (piece,) = by_rows(
+            residual_body, "residual", (jnp.bfloat16,), *sums, targets, earlier=tangent_terms
+        )
+        tangent_sums = self.sums(tangent_terms, (piece,))
+
+        def tangent(*earlier):
+            (tangent_piece,) = by_rows(
+                tangent_body, "tangent_res", (jnp.bfloat16,), *tangent_sums, earlier=earlier
+            )
+            return tangent_piece, both_halves(tangent_piece)
+
+        return both_halves(piece), tangent
 
 
 class Gathers:
@@ -204,11 +267,14 @@
     def inputs(self, tokens, targets):
         return self.whole(tokens), targets
 
-    def residual(self, term, source, targets=None):
-        total = lax.psum_scatter(term(source), "tensor", scatter_dimension=0, tiled=True)
-        if targets is not None:
-            total = total - targets.astype(jnp.float32)
-        return self.whole(total.astype(jnp.bfloat16))
+    def residuals(self, term, hidden, tangent_hidden, targets, earlier):
+        first, second = (
+            lax.psum_scatter(term(source), "tensor", scatter_dimension=0, tiled=True)
+            for source in (hidden, tangent_hidden)
+        )
+        residual = (first - targets.astype(jnp.float32)).astype(jnp.bfloat16)
+        tangent_piece = second.astype(jnp.bfloat16)
+        return self.whole(residual), lambda *earlier: (tangent_piece, self.whole(tangent_piece))
 
 
 def ring_order(count):
@@ -241,12 +307,12 @@
     whole = put(whole, block, 0)
     ahead = behind = block
     full_steps = (count - 1) // 2
-    near_end = block
+    first_block = block
     for step in range(1, full_steps + 1):
         ahead = send(ahead, onward)
         behind = send(behind, back)
-        if step == full_steps - 1:
-            near_end = ahead
+        if step == 1:
+            first_block = ahead
         whole = put(whole, ahead, -step)
         whole = put(whole, behind, step)
     if count % 2 == 0:
@@ -255,7 +321,7 @@
         second = lax.slice_in_dim(behind, half, extent, axis=axis)
         whole = put(whole, send(first, onward), -(full_steps + 1))
         whole = put(whole, send(second, back), full_steps + 1, half)
-    return whole, near_end
+    return whole, first_block
 
 
 def link_matrix(neighbours, numerators):
@@ -294,7 +360,6 @@
         return found
 
 
-LAG = 2
 STEPS = 2
 
 
@@ -326,7 +391,8 @@
         put["made"] = made.astype(jnp.bfloat16)
     if "cross_own" in got:
         put["cross"] = weighted(4, "cross_own", "cross_swapped", "cross_middle").astype(jnp.bfloat16)
-        put["pass_swapped"] = got["cross_swapped"][...]
+    if "pass_swapped" in got:
+        put["pass_swapped"] = got["pass_swapped"][...]
     if "pass_far" in got:
         put["pass_far"] = got["pass_far"][...]
     if "out_middle" in got:
@@ -335,7 +401,10 @@
     for result in results:
         if result != "mixed":
             offset = 0
-            for piece in result.split(":")[1].split("+"):
+            for at, piece in enumerate(result.split(":")[1].split("+")):
+                if len(got[result].shape) == 3:
+                    got[result][at] = put[piece]
+                    continue
                 rows = put[piece].shape[0]
                 start = pl.multiple_of(offset + step * rows, rows)
                 got[result][pl.ds(start, rows), :] = put[piece]
@@ -347,97 +416,133 @@
 
 
 class Pipeline:
-    def __init__(self, links, full_rows, width):
-        me = lax.axis_index("replica")
-        self.scales = jnp.sum(jnp.asarray(Grid.picks())[me] * links, axis=(1, 2))
+    def __init__(self, scales, full_rows, width):
+        self.scales = scales
         self.full_rows, self.width = full_rows, width
         self.place = {}
+        self.received = {}
         self.last = None
 
     def parts(self, count):
         unit = self.full_rows // 64
-        head, tail = [2, 2], [2, 2, 1, 1, 1, 1]
+        sizes = [[4] * 16 for _ in range(count)]
+        sizes[0] = [2] * 4 + [4] * 14
+        sizes[-1] = [4] * 15 + [2] * 2
         found = []
-        for which in range(count):
-            ends = (head if which == 0 else []), (tail if which == count - 1 else [])
-            middle = (64 - sum(ends[0]) - sum(ends[1])) // 4
+        for which, units in enumerate(sizes):
             row = 0
-            for size in ends[0] + [4] * middle + ends[1]:
+            for size in units:
                 found.append((which, row, size * unit))
                 row += size * unit
         return found
 
-    def run(self, sources):
-        parts = self.parts(len(sources))
-        mixed = [None] * len(sources)
-        for tick in range(len(parts) + 4 * LAG):
-            self.tick(tick, parts, sources, mixed)
-        return mixed
-
-    def tick(self, tick, parts, sources, mixed):
-        width = self.width
+    def run(self, stepping, tracking):
+        self.sources = [(*stepping, "step"), None]
+        self.before = {}
+        self.order = self.parts(2)
+        self.mixed = [None, None]
+        for tick in range(len(self.order) + 7):
+            if tick == 3:
+                tracked, (first, second) = tracking(self.last)
+                self.sources[1] = (*tracked, "track")
+                self.before = {6: [first], 9: [second]}
+            self.kernel(("outer", "inner"), tick)
+            self.kernel(("across",), tick)
+        return self.mixed
+
+    def kernel(self, ways, tick):
+        width, parts, place, mixed = self.width, self.order, self.place, self.mixed
         count = len(parts)
         names, operands, specs = ["scales"], [self.scales], [pl.BlockSpec(memory_space=pltpu.SMEM)]
-        place = self.place
 
         def row_spec(depth, start, rows):
             block = rows // STEPS
+            assert start % block == 0
             return pl.BlockSpec((block, depth), lambda i: (start // block + i, 0))
 
         def add(name, key):
             array, start = place[key]
+            rows = parts[key[1]][2]
             names.append(name)
             operands.append(array)
-            specs.append(row_spec(width, start, parts[key[1]][2]))
-
-        payloads = {"outer": [], "inner": [], "across": []}
-        flops = 0
-        part = tick - 3 * LAG
-        if 0 <= part < count:
-            add("out_middle", ("middle", part))
-            add("out_far", ("far", part))
-            add("out_wrapped", ("wrapped", part))
-            payloads["outer"].append(("outward", "rest", part))
-        part = tick - 2 * LAG
-        if 0 <= part < count:
-            add("pass_far", ("far", part))
-            payloads["across"].append(("pass_far", "wrapped", part))
-        part = tick - LAG
-        if 0 <= part < count:
-            add("cross_own", ("own", part))
-            add("cross_swapped", ("swapped", part))
-            add("cross_middle", ("middle", part))
-            payloads["inner"].append(("pass_swapped", "far", part))
-            payloads["across"].append(("cross", "sideways", part))
-        part = tick
-        if part < count:
-            which, start, rows = parts[part]
-            tokens_t, grads, base, tracker, kind = sources[which]
-            depth = grads.shape[0]
-            names += ["tokens_t", "grads", "base", "tracker", kind]
-            operands += [tokens_t, grads, base, tracker, self.scales]
-            specs += [
-                row_spec(depth, start, rows),
-                pl.BlockSpec((depth, width), lambda i: (0, 0)),
-                row_spec(width, start, rows),
-                row_spec(width, start, rows),
-                pl.BlockSpec(memory_space=pltpu.SMEM),
-            ]
-            payloads["outer"].append(("made", "swapped", part))
-            payloads["inner"].append(("made", "middle", part))
-            flops += 2 * rows * depth * width
+            if array.ndim == 3:
+                item = start // rows
+                specs.append(pl.BlockSpec((None, rows // STEPS, width), lambda i: (item, i, 0)))
+            else:
+                specs.append(row_spec(width, start, rows))
+
+        def add_earlier(array):
+            names.append("earlier")
+            operands.append(array)
+            specs.append(pl.BlockSpec(memory_space=pl.ANY))
+
+        payloads = {way: [] for way in ways}
+        flops = moved = 0
+        if "inner" in ways:
+            part = tick
+            if part < count:
+                which, start, rows = parts[part]
+                tokens_t, grads, base, tracker, kind = self.sources[which]
+                depth = grads.shape[0]
+                names += ["tokens_t", "grads", "base", "tracker", kind]
+                operands += [tokens_t, grads, base, tracker, self.scales]
+                specs += [
+                    row_spec(depth, start, rows),
+                    pl.BlockSpec((depth, width), lambda i: (0, 0)),
+                    row_spec(width, start, rows),
+                    row_spec(width, start, rows),
+                    pl.BlockSpec(memory_space=pltpu.SMEM),
+                ]
+                payloads["outer"].append(("made", "swapped", part))
+                payloads["inner"].append(("made", "middle", part))
+                flops += 2 * rows * depth * width
+                moved += 2 * rows
+            part = tick - 2
+            if 0 <= part < count:
+                add("pass_swapped", ("swapped", part))
+                payloads["inner"].append(("pass_swapped", "far", part))
+            part = tick - 5
+            if 0 <= part < count:
+                add("out_middle", ("middle", part))
+                add("out_far", ("far", part))
+                add("out_wrapped", ("wrapped", part))
+                payloads["outer"].append(("outward", "rest", part))
+                moved += 2 * parts[part][2]
+            for array in self.before.get(tick, ()):
+                add_earlier(array)
+        else:
+            part = tick - 2
+            if 0 <= part < count:
+                add("cross_own", ("own", part))
+                add("cross_swapped", ("swapped", part))
+                add("cross_middle", ("middle", part))
+                payloads["across"].append(("cross", "sideways", part))
+                moved += 2 * parts[part][2]
+            part = tick - 3
+            if 0 <= part < count:
+                add("pass_far", ("far", part))
+                payloads["across"].append(("pass_far", "wrapped", part))
+            if ("inner", tick - 1) in self.received:
+                add_earlier(self.received["inner", tick - 1])
         results, shapes, out_specs = [], [], []
         ways = [way for way, pieces in payloads.items() if pieces]
-        moved = 0
         for way in ways:
+            payloads[way].sort(key=lambda piece: -parts[piece[2]][2])
             rows = sum(parts[piece[2]][2] for piece in payloads[way])
             moved += 2 * rows
             results.append(way + ":" + "+".join(piece[0] for piece in payloads[way]))
-            shapes.append(jax.ShapeDtypeStruct((rows, width), jnp.bfloat16))
-            out_specs.append(pl.BlockSpec((rows, width), lambda i: (0, 0)))
+            sizes = {parts[piece[2]][2] for piece in payloads[way]}
+            if len(sizes) == 1:
+                items, each = len(payloads[way]), sizes.pop()
+                shapes.append(jax.ShapeDtypeStruct((items, each, width), jnp.bfloat16))
+                out_specs.append(pl.BlockSpec((items, each // STEPS, width), lambda i: (0, i, 0)))
+            else:
+                shapes.append(jax.ShapeDtypeStruct((rows, width), jnp.bfloat16))
+                out_specs.append(pl.BlockSpec((rows, width), lambda i: (0, 0)))
         aliases = {}
-        part = tick - 4 * LAG
-        if 0 <= part < count:
+        part = tick - 7
+        mixing = 0 <= part < count and "inner" not in payloads
+        if mixing:
             for name in ("own", "swapped", "middle", "far", "sideways", "rest"):
                 add(name, (name, part))
             which, start, rows = parts[part]
@@ -450,10 +555,10 @@
             results.append("mixed")
             shapes.append(jax.ShapeDtypeStruct((self.full_rows, width), jnp.bfloat16))
             out_specs.append(row_spec(width, start, rows))
+        if not results:
+            return
         if self.last is not None:
-            names.append("earlier")
-            operands.append(self.last)
-            specs.append(pl.BlockSpec(memory_space=pl.ANY))
+            add_earlier(self.last)
         got = pl.pallas_call(
             functools.partial(
                 tick_kernel, (tuple(names), tuple(results)), 1.0 / math.sqrt(self.full_rows)
@@ -463,17 +568,18 @@
             out_specs=out_specs,
             out_shape=shapes,
             input_output_aliases=aliases,
-            compiler_params=pltpu.CompilerParams(vmem_limit_bytes=VMEM_BYTES),
+            compiler_params=pltpu.CompilerParams(vmem_limit_bytes=TICK_VMEM_BYTES),
             cost_estimate=pl.CostEstimate(
                 flops=flops, bytes_accessed=2 * moved * width, transcendentals=0
             ),
-            name="tick",
+            name="tick_across" if mixing or "across" in ways else "tick",
         )(*operands)
-        if results[-1] == "mixed":
+        if mixing:
             mixed[which] = got[-1]
         for way, payload in zip(ways, got):
             self.last = payload
             received = send(payload, getattr(Grid, way))
+            self.received[way, tick] = received
             start = 0
             for _, name, part in payloads[way]:
                 place[name, part] = (received, start)
@@ -514,8 +620,13 @@
     group = Swaps() if lax.axis_size("tensor") == 4 else Gathers()
     gathered, target_rows = group.inputs(tokens[0], targets[0])
     gathered_t = turned(gathered)
-    up_full, near_end = ring_gather(up_weight, 0)
-    down_full, _ = ring_gather(after(down_weight, near_end), 1)
+    scales = jnp.zeros(1)
+    if lax.axis_size("replica") == 8:
+        scales = jnp.sum(
+            jnp.asarray(Grid.picks())[lax.axis_index("replica")] * links, axis=(1, 2)
+        )
+    up_full, first_block = ring_gather(up_weight, 0)
+    down_full, _ = ring_gather(after(down_weight, first_block, target_rows, gathered_t, scales), 1)
 
     gate_pre = jnp.dot(gathered, weight_now, preferred_element_type=jnp.float32) * inv_width
     probe_pre = jnp.dot(gathered, probe_here, preferred_element_type=jnp.float32) * inv_width
@@ -525,36 +636,49 @@
     slope_one = logistic * (1.0 + gate_pre * (1.0 - logistic))
     slope_two = logistic * (1.0 - logistic) * (2.0 + gate_pre * (1.0 - 2.0 * logistic))
     hidden = (activated * up_pre).astype(jnp.bfloat16)
+    gate_factor = up_pre * slope_one
+    curve_factor = slope_two * probe_pre * up_pre
     tangent_hidden = (slope_one * probe_pre * up_pre).astype(jnp.bfloat16)
 
     def forward_term(source):
         return jnp.dot(source, down_full, preferred_element_type=jnp.float32) * inv_hidden
 
-    def backward_rows(piece):
-        return (
-            lax.dot_general(
-                piece, down_full, (((1,), (1,)), ((), ())), preferred_element_type=jnp.float32
-            )
-            * inv_hidden
+    residual, tangent_sums = group.residuals(
+        forward_term, hidden, tangent_hidden, target_rows, (gate_factor, curve_factor)
+    )
+    grad_hidden, grad_gate = backward(
+        gate_body,
+        "backward_gate",
+        inv_hidden,
+        (jnp.float32, jnp.bfloat16),
+        residual,
+        down_full,
+        gate_factor,
+    )
+
+    def tracking(*earlier):
+        tangent_piece, tangent_res = tangent_sums(*earlier)
+        (tangent_gate,) = backward(
+            tangent_gate_body,
+            "tangent_gate",
+            inv_hidden,
+            (jnp.bfloat16,),
+            tangent_res,
+            down_full,
+            gate_factor,
+            grad_hidden,
+            curve_factor,
         )
-
-    grad_hidden = backward_rows(group.residual(forward_term, hidden, target_rows))
-    grad_gate = (grad_hidden * up_pre * slope_one).astype(jnp.bfloat16)
-
-    tangent_grad = backward_rows(group.residual(forward_term, tangent_hidden))
-    tangent_gate = (
-        (tangent_grad * slope_one + grad_hidden * slope_two * probe_pre) * up_pre
-    ).astype(jnp.bfloat16)
+        return (gathered_t, tangent_gate, probe_here, tracker_now), (tangent_piece, tangent_gate)
 
     stepping = (gathered_t, grad_gate, weight_now, tracker_now)
-    tracking = (gathered_t, tangent_gate, probe_here, tracker_now)
     if lax.axis_size("replica") == 8:
-        pipeline = Pipeline(links, width, weight_now.shape[1])
-        mixed_weights, mixed_tracker = pipeline.run([(*stepping, "step"), (*tracking, "track")])
+        pipeline = Pipeline(scales, width, weight_now.shape[1])
+        mixed_weights, mixed_tracker = pipeline.run(stepping, tracking)
     else:
         mixer = OffsetMixer(links)
         mixed_weights = mixer.mix(update_rows(step_body, "stepped_rows", *stepping))
-        mixed_tracker = mixer.mix(update_rows(track_body, "tracked_rows", *tracking))
+        mixed_tracker = mixer.mix(update_rows(track_body, "tracked_rows", *tracking()[0]))
     return (mixed_weights[None], mixed_tracker[None])
 
 

time: 940 us -> 906 us (0.964)
  local copies, waits for them, and re-layouts: 82.9 us -> 31.8 us
  Pallas kernels: 164 us -> 211 us
  waiting for transfers between devices: 361 us -> 325 us
  starting transfers between devices: 249 us -> 279 us
  matrix products: 47.2 us -> 26.1 us
    unnamed x420 -> x364, local copies, waits for them, and re-layouts: 70.9 us -> 18.4 us
    pallas_call x49 -> x86, Pallas kernels: 163 us -> 209 us  [the longest x80 197 us: kernel(): pl.pallas_call(functools.partial(tick_kernel, (tuple(names), tuple(result...]
    ppermute x137 -> x129, starting transfers between devices: 245 us -> 274 us  [send(): return lax.ppermute(value, 'replica', pairs)]
    ppermute x137 -> x129, waiting for transfers between devices: 325 us -> 306 us  [send(): return lax.ppermute(value, 'replica', pairs)]
    ppermute x3 -> x4, waiting for transfers between devices: 35 us -> 16.7 us  [the longest x2 16.7 us: sums(): lax.ppermute(sent, 'tensor', [(0, 2), (2, 0), (1, 3), (3, 1)])]
    dot_general x2 -> x0, matrix products: 15.6 us -> none  [backward_rows(): lax.dot_general(piece, down_full, (((1,), (1,)), ((), ())), preferred_ele...]
  transfers between devices with their start and end apart: 145 -> 138, of which waited for: 51 -> 76; matrix products, arithmetic and copies ran while one was open for 6% -> 5% of each run, Pallas kernels for 17% -> 22%
where the time goes in v2:
time: 906 us; the launch traced here: 894 us
  waiting for transfers between devices  325 us (36%)
  starting transfers between devices  279 us (31%)
  Pallas kernels  211 us (23%)
  local copies, waits for them, and re-layouts  31.8 us (4%)
  matrix products  26.1 us (3%)
  between operations  16.4 us (2%)
    ppermute x129, waiting for transfers between devices, send(): return lax.ppermute(value, 'replica', pairs)  306 us
    ppermute x129, starting transfers between devices, send(): return lax.ppermute(value, 'replica', pairs)  274 us
    pallas_call x80, Pallas kernels, kernel(): pl.pallas_call(functools.partial(tick_kernel, (tuple(names), tuple(result...  197 us
    unnamed x364, local copies, waits for them, and re-layouts  18.4 us
  transfers between devices with their start and end apart: 138, of which 76 were waited for; matrix products, arithmetic and copies ran while one was open for 5% of the time, Pallas kernels for 22%

profile of v2, /device:TPU:0, one launch (start us, length us, event | category | flops | bytes accessed | tf_op | source)
XLA Modules:
  0.0 894.3 jit_solution(13789891929299930751)
XLA Ops:
  54.7 15.5 %collective-permute-done.11 = bf16[1792,256]{1,0:T(8,128)(2,1)S(1)} collective-permute-done((bf16[1792,256]{1,0:T(8,128)(2,1)S(1)}, bf16[1792,256]{1,0:T(8,128)(2,1)S(1)}, u32[]{:S(2)}, u32[]{:S(2)}) %collective-permute-start.11) | collective-permute-done | bytes 917536 | tf_op jit(solution)/shard_map/ppermute | solution.py:23
  72.6 17.2 %collective-permute-done.6 = bf16[256,1792]{1,0:T(8,128)(2,1)S(1)} collective-permute-done((bf16[256,1792]{1,0:T(8,128)(2,1)S(1)}, bf16[256,1792]{1,0:T(8,128)(2,1)S(1)}, u32[]{:S(2)}, u32[]{:S(2)}) %collective-permute-start.6) | collective-permute-done | bytes 917536 | tf_op jit(solution)/shard_map/ppermute | solution.py:23
  94.1 15.4 %collective-permute-done.13 = bf16[1792,256]{1,0:T(8,128)(2,1)S(1)} collective-permute-done((bf16[1792,256]{1,0:T(8,128)(2,1)S(1)}, bf16[1792,256]{1,0:T(8,128)(2,1)S(1)}, u32[]{:S(2)}, u32[]{:S(2)}) %collective-permute-start.13) | collective-permute-done | bytes 917536 | tf_op jit(solution)/shard_map/ppermute | solution.py:23
  111.9 7.4 collective-permute-done.8
  122.3 10.3 %fusion.4 = (f32[384,1792]{1,0:T(8,128)S(1)}, bf16[384,1792]{1,0:T(8,128)(2,1)}, f32[384,1792]{1,0:T(8,128)S(1)}, bf16[384,1792]{1,0:T(8,128)(2,1)}) fusion(f32[384,1792]{1,0:T(8,128)} %convolution_multiply_fusion.1, f32[384,1792]{1,0:T(8,128)} %convolution_multiply_fusion.2, bf16[2048,1792]{1,0:T(8,128)(2,1)} %constant_dynamic-update-slice_fusion.8, ...), kind=kOutput, calls=%fused_computation.9 | convolution fusion | flops 2839117824 | bytes 22675456 | tf_op jit(solution)/shard_map/dot_general | solution.py:633
  132.6 6.0 collective-permute-done.15
  141.4 9.7 %collective-permute-done.17 = bf16[1792,128]{1,0:T(8,128)(2,1)S(1)} collective-permute-done((bf16[1792,128]{1,0:T(8,128)(2,1)S(1)}, bf16[1792,128]{1,0:T(8,128)(2,1)S(1)}, u32[]{:S(2)}, u32[]{:S(2)}) %collective-permute-start.17) | collective-permute-done | bytes 458784 | tf_op jit(solution)/shard_map/ppermute | solution.py:23
  162.3 16.7 %collective-permute-done.21.refs_1_ = bf16[192,2048]{1,0:T(8,128)(2,1)S(1)} collective-permute-done((bf16[192,2048]{1,0:T(8,128)(2,1)S(1)}, bf16[192,2048]{1,0:T(8,128)(2,1)S(1)}, u32[]{:S(2)}, u32[]{:S(2)}) %collective-permute-start.21) | collective-permute-done | bytes 786464 | tf_op jit(solution)/shard_map/ppermute | solution.py:244
  201.3 8.9 collective-permute-start.29
  211.1 5.7 collective-permute-done.29.refs_6_.refs_2_.refs_7_
  228.1 12.7 %collective-permute-start.34 = (bf16[1,64,1792]{2,1,0:T(8,128)(2,1)S(1)}, bf16[1,64,1792]{2,1,0:T(8,128)(2,1)S(1)}, u32[]{:S(2)}, u32[]{:S(2)}) collective-permute-start(bf16[1,64,1792]{2,1,0:T(8,128)(2,1)S(1)} %get-tuple-element.159.refs_1_.refs_6_), channel_id=1, source_target_pairs={{0,8},{4,12},{8,0},{12,4},{16,24},{20,28},{24,16},{28,20},{1,9},{5... | collective-permute-start | bytes 688136 | tf_op jit(solution)/shard_map/ppermute | solution.py:23
  244.8 14.4 %collective-permute-start.31 = (bf16[1,128,1792]{2,1,0:T(8,128)(2,1)S(1)}, bf16[1,128,1792]{2,1,0:T(8,128)(2,1)S(1)}, u32[]{:S(2)}, u32[]{:S(2)}) collective-permute-start(bf16[1,128,1792]{2,1,0:T(8,128)(2,1)S(1)} %get-tuple-element.157.refs_1_.refs_6_), channel_id=1, source_target_pairs={{0,8},{4,12},{8,0},{12,4},{16,24},{20,28},{24,16},{28,20},{1,9},{5... | collective-permute-start | bytes 1376264 | tf_op jit(solution)/shard_map/ppermute | solution.py:23
  294.2 9.3 %collective-permute-done.37.refs_6_.refs_2_.refs_11_.refs_7_ = bf16[192,1792]{1,0:T(8,128)(2,1)S(1)} collective-permute-done((bf16[192,1792]{1,0:T(8,128)(2,1)S(1)}, bf16[192,1792]{1,0:T(8,128)(2,1)S(1)}, u32[]{:S(2)}, u32[]{:S(2)}) %collective-permute-start.37) | collective-permute-done | bytes 688160 | tf_op jit(solution)/shard_map/ppermute | solution.py:23
  317.5 8.6 collective-permute-start.44
  358.0 5.7 collective-permute-done.53.refs_6_.refs_2_.refs_11_.refs_7_
  569.4 5.1 collective-permute-start.88
  667.7 5.4 collective-permute-start.98
  766.0 5.0 collective-permute-start.119
  809.0 11.9 %collective-permute-start.126 = (bf16[192,1792]{1,0:T(8,128)(2,1)}, bf16[192,1792]{1,0:T(8,128)(2,1)S(1)}, u32[]{:S(2)}, u32[]{:S(2)}) collective-permute-start(bf16[192,1792]{1,0:T(8,128)(2,1)} %get-tuple-element.274.refs_1_), channel_id=1, source_target_pairs={{0,8},{4,12},{8,0},{12,4},{16,24},{20,28},{24,16},{28,20},{1,9},{5... | collective-permute-start | bytes 2064392 | tf_op jit(solution)/shard_map/ppermute | solution.py:23
  827.7 7.4 collective-permute-start.122
  835.4 5.0 collective-permute-done.127.refs_4_.refs_5_
  845.7 5.4 collective-permute-start.131
  851.1 9.0 %collective-permute-done.125.refs_4_.refs_5_ = bf16[2,128,1792]{2,1,0:T(8,128)(2,1)S(1)} collective-permute-done((bf16[2,128,1792]{2,1,0:T(8,128)(2,1)S(1)}, bf16[2,128,1792]{2,1,0:T(8,128)(2,1)S(1)}, u32[]{:S(2)}, u32[]{:S(2)}) %collective-permute-start.125) | collective-permute-done | bytes 917536 | tf_op jit(solution)/shard_map/ppermute | solution.py:23
  865.5 5.3 collective-permute-start.137
  (753 shorter events, 654.9 us)
Async XLA Ops:
  34.6 35.6 %collective-permute-start.11 = (bf16[1792,256]{1,0:T(8,128)(2,1)S(1)}, bf16[1792,256]{1,0:T(8,128)(2,1)S(1)}, u32[]{:S(2)}, u32[]{:S(2)}) collective-permute-start(bf16[1792,256]{1,0:T(8,128)(2,1)S(1)} %after.1), channel_id=1, source_target_pairs={{0,8},{8,16},{16,24},{24,28},{28,20},{20,12},{12,4},{4,0},{1,9},{9... | collective-permute-start | bytes 2752520 | tf_op jit(solution)/shard_map/ppermute | solution.py:23
  36.7 35.7 %collective-permute-start.12 = (bf16[1792,256]{1,0:T(8,128)(2,1)S(1)}, bf16[1792,256]{1,0:T(8,128)(2,1)S(1)}, u32[]{:S(2)}, u32[]{:S(2)}) collective-permute-start(bf16[1792,256]{1,0:T(8,128)(2,1)S(1)} %after.1), channel_id=1, source_target_pairs={{8,0},{16,8},{24,16},{28,24},{20,28},{12,20},{4,12},{0,4},{9,1},{1... | collective-permute-start | bytes 2752520 | tf_op jit(solution)/shard_map/ppermute | solution.py:23
  50.5 39.3 %collective-permute-start.6 = (bf16[256,1792]{1,0:T(8,128)(2,1)S(1)}, bf16[256,1792]{1,0:T(8,128)(2,1)S(1)}, u32[]{:S(2)}, u32[]{:S(2)}) collective-permute-start(bf16[256,1792]{1,0:T(8,128)(2,1)S(1)} %collective-permute-done.4), channel_id=1, source_target_pairs={{0,8},{8,16},{16,24},{24,28},{28,20},{20,12},{12,4},{4,0},{1,9},{9... | collective-permute-start | bytes 2752520 | tf_op jit(solution)/shard_map/ppermute | solution.py:23
  52.7 39.3 %collective-permute-start.7 = (bf16[256,1792]{1,0:T(8,128)(2,1)S(1)}, bf16[256,1792]{1,0:T(8,128)(2,1)S(1)}, u32[]{:S(2)}, u32[]{:S(2)}) collective-permute-start(bf16[256,1792]{1,0:T(8,128)(2,1)S(1)} %collective-permute-done.5), channel_id=1, source_target_pairs={{8,0},{16,8},{24,16},{28,24},{20,28},{12,20},{4,12},{0,4},{9,1},{1... | collective-permute-start | bytes 2752520 | tf_op jit(solution)/shard_map/ppermute | solution.py:23
  70.1 39.3 %collective-permute-start.13 = (bf16[1792,256]{1,0:T(8,128)(2,1)S(1)}, bf16[1792,256]{1,0:T(8,128)(2,1)S(1)}, u32[]{:S(2)}, u32[]{:S(2)}) collective-permute-start(bf16[1792,256]{1,0:T(8,128)(2,1)S(1)} %collective-permute-done.11), channel_id=1, source_target_pairs={{0,8},{8,16},{16,24},{24,28},{28,20},{20,12},{12,4},{4,0},{1,9},{9... | collective-permute-start | bytes 2752520 | tf_op jit(solution)/shard_map/ppermute | solution.py:23
  72.3 39.3 %collective-permute-start.14 = (bf16[1792,256]{1,0:T(8,128)(2,1)S(1)}, bf16[1792,256]{1,0:T(8,128)(2,1)S(1)}, u32[]{:S(2)}, u32[]{:S(2)}) collective-permute-start(bf16[1792,256]{1,0:T(8,128)(2,1)S(1)} %collective-permute-done.12), channel_id=1, source_target_pairs={{8,0},{16,8},{24,16},{28,24},{20,28},{12,20},{4,12},{0,4},{9,1},{1... | collective-permute-start | bytes 2752520 | tf_op jit(solution)/shard_map/ppermute | solution.py:23
  222.1 40.0 %collective-permute-start.35 = (bf16[192,1792]{1,0:T(8,128)(2,1)}, bf16[192,1792]{1,0:T(8,128)(2,1)S(1)}, u32[]{:S(2)}, u32[]{:S(2)}) collective-permute-start(bf16[192,1792]{1,0:T(8,128)(2,1)} %get-tuple-element.158.refs_6_), channel_id=1, source_target_pairs={{8,16},{12,20},{16,8},{20,12},{9,17},{13,21},{17,9},{21,13},{10,18... | collective-permute-start | bytes 2064392 | tf_op jit(solution)/shard_map/ppermute | solution.py:23
  226.2 39.5 %collective-permute-start.22 = (bf16[192,2048]{1,0:T(8,128)(2,1)}, bf16[192,2048]{1,0:T(8,128)(2,1)S(1)}, u32[]{:S(2)}, u32[]{:S(2)}) collective-permute-start(bf16[192,2048]{1,0:T(8,128)(2,1)} %get-tuple-element.147), channel_id=1, source_target_pairs={{0,2},{2,0},{1,3},{3,1},{4,6},{6,4},{5,7},{7,5},{8,10},{10,8},{9,1... | collective-permute-start | bytes 2359304 | tf_op jit(solution)/shard_map/ppermute | solution.py:244
  227.8 31.4 %collective-permute-start.36 = (bf16[2,64,1792]{2,1,0:T(8,128)(2,1)S(1)}, bf16[2,64,1792]{2,1,0:T(8,128)(2,1)S(1)}, u32[]{:S(2)}, u32[]{:S(2)}) collective-permute-start(bf16[2,64,1792]{2,1,0:T(8,128)(2,1)S(1)} %tick_across.41.refs_7_), channel_id=1, source_target_pairs={{0,4},{4,0},{8,12},{12,8},{16,20},{20,16},{24,28},{28,24},{1,5},{5... | collective-permute-start | bytes 1376264 | tf_op jit(solution)/shard_map/ppermute | solution.py:23
  293.8 41.8 %collective-permute-start.49 = (bf16[2,128,1792]{2,1,0:T(8,128)(2,1)}, bf16[2,128,1792]{2,1,0:T(8,128)(2,1)}, u32[]{:S(2)}, u32[]{:S(2)}) collective-permute-start(bf16[2,128,1792]{2,1,0:T(8,128)(2,1)} %get-tuple-element.165.refs_10_), channel_id=1, source_target_pairs={{0,4},{4,0},{8,12},{12,8},{16,20},{20,16},{24,28},{28,24},{1,5},{5... | collective-permute-start | bytes 2752520 | tf_op jit(solution)/shard_map/ppermute | solution.py:23
  303.5 31.2 %collective-permute-start.47 = (bf16[192,1792]{1,0:T(8,128)(2,1)}, bf16[192,1792]{1,0:T(8,128)(2,1)S(1)}, u32[]{:S(2)}, u32[]{:S(2)}) collective-permute-start(bf16[192,1792]{1,0:T(8,128)(2,1)} %get-tuple-element.170.refs_1_.refs_6_), channel_id=1, source_target_pairs={{0,8},{4,12},{8,0},{12,4},{16,24},{20,28},{24,16},{28,20},{1,9},{5... | collective-permute-start | bytes 2064392 | tf_op jit(solution)/shard_map/ppermute | solution.py:23
  311.8 31.1 %collective-permute-start.48 = (bf16[2,128,1792]{2,1,0:T(8,128)(2,1)}, bf16[2,128,1792]{2,1,0:T(8,128)(2,1)S(1)}, u32[]{:S(2)}, u32[]{:S(2)}) collective-permute-start(bf16[2,128,1792]{2,1,0:T(8,128)(2,1)} %get-tuple-element.168.refs_13_), channel_id=1, source_target_pairs={{8,16},{12,20},{16,8},{20,12},{9,17},{13,21},{17,9},{21,13},{10,18... | collective-permute-start | bytes 2752520 | tf_op jit(solution)/shard_map/ppermute | solution.py:23
  314.5 32.1 %collective-permute-start.46 = (bf16[2,128,1792]{2,1,0:T(8,128)(2,1)}, bf16[2,128,1792]{2,1,0:T(8,128)(2,1)S(1)}, u32[]{:S(2)}, u32[]{:S(2)}) collective-permute-start(bf16[2,128,1792]{2,1,0:T(8,128)(2,1)} %get-tuple-element.169.refs_11_), channel_id=1, source_target_pairs={{0,4},{4,0},{8,12},{12,8},{16,20},{20,16},{24,28},{28,24},{1,5},{5... | collective-permute-start | bytes 2752520 | tf_op jit(solution)/shard_map/ppermute | solution.py:23
  352.6 30.7 %collective-permute-start.50 = (bf16[2,128,1792]{2,1,0:T(8,128)(2,1)S(1)}, bf16[2,128,1792]{2,1,0:T(8,128)(2,1)S(1)}, u32[]{:S(2)}, u32[]{:S(2)}) collective-permute-start(bf16[2,128,1792]{2,1,0:T(8,128)(2,1)S(1)} %get-tuple-element.174.refs_1_.refs_6_), channel_id=1, source_target_pairs={{0,8},{4,12},{8,0},{12,4},{16,24},{20,28},{24,16},{28,20},{1,9},{5... | collective-permute-start | bytes 2752520 | tf_op jit(solution)/shard_map/ppermute | solution.py:23
  357.0 31.3 %collective-permute-start.52 = (bf16[2,128,1792]{2,1,0:T(8,128)(2,1)}, bf16[2,128,1792]{2,1,0:T(8,128)(2,1)S(1)}, u32[]{:S(2)}, u32[]{:S(2)}) collective-permute-start(bf16[2,128,1792]{2,1,0:T(8,128)(2,1)} %get-tuple-element.177.refs_10_), channel_id=1, source_target_pairs={{0,4},{4,0},{8,12},{12,8},{16,20},{20,16},{24,28},{28,24},{1,5},{5... | collective-permute-start | bytes 2752520 | tf_op jit(solution)/shard_map/ppermute | solution.py:23
  451.2 30.4 %collective-permute-start.71 = (bf16[2,128,1792]{2,1,0:T(8,128)(2,1)}, bf16[2,128,1792]{2,1,0:T(8,128)(2,1)S(1)}, u32[]{:S(2)}, u32[]{:S(2)}) collective-permute-start(bf16[2,128,1792]{2,1,0:T(8,128)(2,1)} %get-tuple-element.202.refs_1_.refs_6_), channel_id=1, source_target_pairs={{0,8},{4,12},{8,0},{12,4},{16,24},{20,28},{24,16},{28,20},{1,9},{5... | collective-permute-start | bytes 2752520 | tf_op jit(solution)/shard_map/ppermute | solution.py:23
  549.6 30.4 %collective-permute-start.80 = (bf16[2,128,1792]{2,1,0:T(8,128)(2,1)}, bf16[2,128,1792]{2,1,0:T(8,128)(2,1)S(1)}, u32[]{:S(2)}, u32[]{:S(2)}) collective-permute-start(bf16[2,128,1792]{2,1,0:T(8,128)(2,1)} %get-tuple-element.214.refs_1_.refs_6_), channel_id=1, source_target_pairs={{0,8},{4,12},{8,0},{12,4},{16,24},{20,28},{24,16},{28,20},{1,9},{5... | collective-permute-start | bytes 2752520 | tf_op jit(solution)/shard_map/ppermute | solution.py:23
  647.2 31.0 %collective-permute-start.101 = (bf16[2,128,1792]{2,1,0:T(8,128)(2,1)S(1)}, bf16[2,128,1792]{2,1,0:T(8,128)(2,1)S(1)}, u32[]{:S(2)}, u32[]{:S(2)}) collective-permute-start(bf16[2,128,1792]{2,1,0:T(8,128)(2,1)S(1)} %get-tuple-element.242.refs_1_.refs_6_), channel_id=1, source_target_pairs={{0,8},{4,12},{8,0},{12,4},{16,24},{20,28},{24,16},{28,20},{1,9},{5... | collective-permute-start | bytes 2752520 | tf_op jit(solution)/shard_map/ppermute | solution.py:23
  706.9 30.4 %collective-permute-start.104 = (bf16[2,128,1792]{2,1,0:T(8,128)(2,1)S(1)}, bf16[2,128,1792]{2,1,0:T(8,128)(2,1)S(1)}, u32[]{:S(2)}, u32[]{:S(2)}) collective-permute-start(bf16[2,128,1792]{2,1,0:T(8,128)(2,1)S(1)} %get-tuple-element.246.refs_1_.refs_6_), channel_id=1, source_target_pairs={{0,8},{4,12},{8,0},{12,4},{16,24},{20,28},{24,16},{28,20},{1,9},{5... | collective-permute-start | bytes 2752520 | tf_op jit(solution)/shard_map/ppermute | solution.py:23
  785.8 35.1 %collective-permute-start.116 = (bf16[2,128,1792]{2,1,0:T(8,128)(2,1)S(1)}, bf16[2,128,1792]{2,1,0:T(8,128)(2,1)S(1)}, u32[]{:S(2)}, u32[]{:S(2)}) collective-permute-start(bf16[2,128,1792]{2,1,0:T(8,128)(2,1)S(1)} %get-tuple-element.262.refs_1_), channel_id=1, source_target_pairs={{0,8},{4,12},{8,0},{12,4},{16,24},{20,28},{24,16},{28,20},{1,9},{5... | collective-permute-start | bytes 2752520 | tf_op jit(solution)/shard_map/ppermute | solution.py:23
  807.6 32.9 %collective-permute-start.127 = (bf16[2,128,1792]{2,1,0:T(8,128)(2,1)}, bf16[2,128,1792]{2,1,0:T(8,128)(2,1)S(1)}, u32[]{:S(2)}, u32[]{:S(2)}) collective-permute-start(bf16[2,128,1792]{2,1,0:T(8,128)(2,1)} %get-tuple-element.269.refs_10_), channel_id=1, source_target_pairs={{0,4},{4,0},{8,12},{12,8},{16,20},{20,16},{24,28},{28,24},{1,5},{5... | collective-permute-start | bytes 2752520 | tf_op jit(solution)/shard_map/ppermute | solution.py:23
  826.4 33.8 %collective-permute-start.125 = (bf16[2,128,1792]{2,1,0:T(8,128)(2,1)S(1)}, bf16[2,128,1792]{2,1,0:T(8,128)(2,1)S(1)}, u32[]{:S(2)}, u32[]{:S(2)}) collective-permute-start(bf16[2,128,1792]{2,1,0:T(8,128)(2,1)S(1)} %get-tuple-element.273.refs_5_), channel_id=1, source_target_pairs={{0,4},{4,0},{8,12},{12,8},{16,20},{20,16},{24,28},{28,24},{1,5},{5... | collective-permute-start | bytes 2752520 | tf_op jit(solution)/shard_map/ppermute | solution.py:23
  843.6 31.2 %collective-permute-start.132 = (bf16[192,1792]{1,0:T(8,128)(2,1)S(1)}, bf16[192,1792]{1,0:T(8,128)(2,1)S(1)}, u32[]{:S(2)}, u32[]{:S(2)}) collective-permute-start(bf16[192,1792]{1,0:T(8,128)(2,1)S(1)} %get-tuple-element.277.refs_5_), channel_id=1, source_target_pairs={{0,4},{4,0},{8,12},{12,8},{16,20},{20,16},{24,28},{28,24},{1,5},{5... | collective-permute-start | bytes 2064392 | tf_op jit(solution)/shard_map/ppermute | solution.py:23
  845.7 31.5 %collective-permute-start.131 = (bf16[1,128,1792]{2,1,0:T(8,128)(2,1)S(1)}, bf16[1,128,1792]{2,1,0:T(8,128)(2,1)S(1)}, u32[]{:S(2)}, u32[]{:S(2)}) collective-permute-start(bf16[1,128,1792]{2,1,0:T(8,128)(2,1)S(1)} %get-tuple-element.281), channel_id=1, source_target_pairs={{0,8},{4,12},{8,0},{12,4},{16,24},{20,28},{24,16},{28,20},{1,9},{5... | collective-permute-start | bytes 1376264 | tf_op jit(solution)/shard_map/ppermute | solution.py:23
  (295 other events, 5050.1 us)

commit v3 on v2

--- a/solution.py
+++ b/solution.py
@@ -426,7 +426,7 @@
     def parts(self, count):
         unit = self.full_rows // 64
         sizes = [[4] * 16 for _ in range(count)]
-        sizes[0] = [2] * 4 + [4] * 14
+        sizes[0] = [4] * 16
         sizes[-1] = [4] * 15 + [2] * 2
         found = []
         for which, units in enumerate(sizes):

time: 906 us -> 915 us (level)
  starting transfers between devices: 279 us -> 327 us
  waiting for transfers between devices: 325 us -> 285 us
    ppermute x129 -> x123, starting transfers between devices: 274 us -> 322 us  [send(): return lax.ppermute(value, 'replica', pairs)]
    ppermute x129 -> x123, waiting for transfers between devices: 306 us -> 266 us  [send(): return lax.ppermute(value, 'replica', pairs)]
    unnamed x364 -> x332, local copies, waits for them, and re-layouts: 18.4 us -> 21.6 us
    pallas_call x80 -> x76, Pallas kernels: 197 us -> 194 us  [kernel(): pl.pallas_call(functools.partial(tick_kernel, (tuple(names), tuple(result...]
  transfers between devices with their start and end apart: 138 -> 132, of which waited for: 76 -> 47; matrix products, arithmetic and copies ran while one was open for 5% -> 5% of each run, Pallas kernels for 22% -> 22%
where the time goes in v3:
time: 915 us; the launch traced here: 904 us
  starting transfers between devices  327 us (36%)
  waiting for transfers between devices  285 us (31%)
  Pallas kernels  206 us (23%)
  local copies, waits for them, and re-layouts  36.7 us (4%)
  matrix products  26.3 us (3%)
  between operations  16.3 us (2%)
    ppermute x123, starting transfers between devices, send(): return lax.ppermute(value, 'replica', pairs)  322 us
    ppermute x123, waiting for transfers between devices, send(): return lax.ppermute(value, 'replica', pairs)  266 us
    pallas_call x76, Pallas kernels, kernel(): pl.pallas_call(functools.partial(tick_kernel, (tuple(names), tuple(result...  194 us
    unnamed x332, local copies, waits for them, and re-layouts  21.6 us
  transfers between devices with their start and end apart: 132, of which 47 were waited for; matrix products, arithmetic and copies ran while one was open for 5% of the time, Pallas kernels for 22%

profile of v3, /device:TPU:0, one launch (start us, length us, event | category | flops | bytes accessed | tf_op | source)
XLA Modules:
  0.0 903.6 jit_solution(8242882518685696017)
XLA Ops:
  56.0 15.7 %collective-permute-done.12 = bf16[1792,256]{1,0:T(8,128)(2,1)S(1)} collective-permute-done((bf16[1792,256]{1,0:T(8,128)(2,1)S(1)}, bf16[1792,256]{1,0:T(8,128)(2,1)S(1)}, u32[]{:S(2)}, u32[]{:S(2)}) %collective-permute-start.12) | collective-permute-done | bytes 917536 | tf_op jit(solution)/shard_map/ppermute | solution.py:23
  74.0 17.4 %collective-permute-done.7 = bf16[256,1792]{1,0:T(8,128)(2,1)S(1)} collective-permute-done((bf16[256,1792]{1,0:T(8,128)(2,1)S(1)}, bf16[256,1792]{1,0:T(8,128)(2,1)S(1)}, u32[]{:S(2)}, u32[]{:S(2)}) %collective-permute-start.7) | collective-permute-done | bytes 917536 | tf_op jit(solution)/shard_map/ppermute | solution.py:23
  95.5 15.6 %collective-permute-done.14 = bf16[1792,256]{1,0:T(8,128)(2,1)} collective-permute-done((bf16[1792,256]{1,0:T(8,128)(2,1)S(1)}, bf16[1792,256]{1,0:T(8,128)(2,1)}, u32[]{:S(2)}, u32[]{:S(2)}) %collective-permute-start.14) | collective-permute-done | bytes 917536 | tf_op jit(solution)/shard_map/ppermute | solution.py:23
  124.1 10.4 %fusion.4 = (f32[384,1792]{1,0:T(8,128)S(1)}, bf16[384,1792]{1,0:T(8,128)(2,1)}, f32[384,1792]{1,0:T(8,128)S(1)}, bf16[384,1792]{1,0:T(8,128)(2,1)}) fusion(f32[384,1792]{1,0:T(8,128)} %convolution_multiply_fusion.1, f32[384,1792]{1,0:T(8,128)} %convolution_multiply_fusion.2, bf16[2048,1792]{1,0:T(8,128)(2,1)} %constant_dynamic-update-slice_fusion.8, ...), kind=kOutput, calls=%fused_computation.9 | convolution fusion | flops 2839117824 | bytes 22675456 | tf_op jit(solution)/shard_map/dot_general | solution.py:633
  142.9 11.2 %collective-permute-done.17 = bf16[1792,128]{1,0:T(8,128)(2,1)S(1)} collective-permute-done((bf16[1792,128]{1,0:T(8,128)(2,1)S(1)}, bf16[1792,128]{1,0:T(8,128)(2,1)S(1)}, u32[]{:S(2)}, u32[]{:S(2)}) %collective-permute-start.17) | collective-permute-done | bytes 458784 | tf_op jit(solution)/shard_map/ppermute | solution.py:23
  163.9 16.7 %collective-permute-done.21.refs_1_ = bf16[192,2048]{1,0:T(8,128)(2,1)S(1)} collective-permute-done((bf16[192,2048]{1,0:T(8,128)(2,1)S(1)}, bf16[192,2048]{1,0:T(8,128)(2,1)S(1)}, u32[]{:S(2)}, u32[]{:S(2)}) %collective-permute-start.21) | collective-permute-done | bytes 786464 | tf_op jit(solution)/shard_map/ppermute | solution.py:244
  193.9 10.4 %collective-permute-done.24.refs_6_.refs_2_.refs_7_ = bf16[1,128,1792]{2,1,0:T(8,128)(2,1)S(1)} collective-permute-done((bf16[1,128,1792]{2,1,0:T(8,128)(2,1)S(1)}, bf16[1,128,1792]{2,1,0:T(8,128)(2,1)S(1)}, u32[]{:S(2)}, u32[]{:S(2)}) %collective-permute-start.24) | collective-permute-done | bytes 458784 | tf_op jit(solution)/shard_map/ppermute | solution.py:23
  217.1 10.4 %collective-permute-done.29.refs_6_.refs_2_.refs_7_ = bf16[1,128,1792]{2,1,0:T(8,128)(2,1)S(1)} collective-permute-done((bf16[1,128,1792]{2,1,0:T(8,128)(2,1)S(1)}, bf16[1,128,1792]{2,1,0:T(8,128)(2,1)S(1)}, u32[]{:S(2)}, u32[]{:S(2)}) %collective-permute-start.29) | collective-permute-done | bytes 458784 | tf_op jit(solution)/shard_map/ppermute | solution.py:23
  238.5 27.2 %collective-permute-start.34 = (bf16[1,128,1792]{2,1,0:T(8,128)(2,1)S(1)}, bf16[1,128,1792]{2,1,0:T(8,128)(2,1)S(1)}, u32[]{:S(2)}, u32[]{:S(2)}) collective-permute-start(bf16[1,128,1792]{2,1,0:T(8,128)(2,1)S(1)} %get-tuple-element.151.refs_1_.refs_6_), channel_id=1, source_target_pairs={{0,8},{4,12},{8,0},{12,4},{16,24},{20,28},{24,16},{28,20},{1,9},{5... | collective-permute-start | bytes 1376264 | tf_op jit(solution)/shard_map/ppermute | solution.py:23
  279.3 22.8 %collective-permute-start.31 = (bf16[1,128,1792]{2,1,0:T(8,128)(2,1)S(1)}, bf16[1,128,1792]{2,1,0:T(8,128)(2,1)S(1)}, u32[]{:S(2)}, u32[]{:S(2)}) collective-permute-start(bf16[1,128,1792]{2,1,0:T(8,128)(2,1)S(1)} %get-tuple-element.149.refs_1_.refs_6_), channel_id=1, source_target_pairs={{0,8},{4,12},{8,0},{12,4},{16,24},{20,28},{24,16},{28,20},{1,9},{5... | collective-permute-start | bytes 1376264 | tf_op jit(solution)/shard_map/ppermute | solution.py:23
  302.4 11.2 %collective-permute-done.31.refs_6_.refs_2_.refs_7_ = bf16[1,128,1792]{2,1,0:T(8,128)(2,1)S(1)} collective-permute-done((bf16[1,128,1792]{2,1,0:T(8,128)(2,1)S(1)}, bf16[1,128,1792]{2,1,0:T(8,128)(2,1)S(1)}, u32[]{:S(2)}, u32[]{:S(2)}) %collective-permute-start.31) | collective-permute-done | bytes 458784 | tf_op jit(solution)/shard_map/ppermute | solution.py:23
  400.0 12.7 %collective-permute-start.50 = (bf16[2,128,1792]{2,1,0:T(8,128)(2,1)S(1)}, bf16[2,128,1792]{2,1,0:T(8,128)(2,1)S(1)}, u32[]{:S(2)}, u32[]{:S(2)}) collective-permute-start(bf16[2,128,1792]{2,1,0:T(8,128)(2,1)S(1)} %get-tuple-element.166.refs_1_.refs_6_), channel_id=1, source_target_pairs={{0,8},{4,12},{8,0},{12,4},{16,24},{20,28},{24,16},{28,20},{1,9},{5... | collective-permute-start | bytes 2752520 | tf_op jit(solution)/shard_map/ppermute | solution.py:23
  423.9 8.9 collective-permute-start.59
  503.6 9.7 %collective-permute-done.64.refs_9_.refs_10_ = bf16[2,128,1792]{2,1,0:T(8,128)(2,1)S(1)} collective-permute-done((bf16[2,128,1792]{2,1,0:T(8,128)(2,1)}, bf16[2,128,1792]{2,1,0:T(8,128)(2,1)S(1)}, u32[]{:S(2)}, u32[]{:S(2)}) %collective-permute-start.64) | collective-permute-done | bytes 917536 | tf_op jit(solution)/shard_map/ppermute | solution.py:23
  541.3 8.9 collective-permute-start.77
  562.5 9.7 %collective-permute-done.79.refs_9_.refs_10_ = bf16[2,128,1792]{2,1,0:T(8,128)(2,1)S(1)} collective-permute-done((bf16[2,128,1792]{2,1,0:T(8,128)(2,1)}, bf16[2,128,1792]{2,1,0:T(8,128)(2,1)S(1)}, u32[]{:S(2)}, u32[]{:S(2)}) %collective-permute-start.79) | collective-permute-done | bytes 917536 | tf_op jit(solution)/shard_map/ppermute | solution.py:23
  600.4 8.9 collective-permute-start.80
  622.0 9.2 %collective-permute-done.86.refs_9_.refs_10_ = bf16[2,128,1792]{2,1,0:T(8,128)(2,1)S(1)} collective-permute-done((bf16[2,128,1792]{2,1,0:T(8,128)(2,1)}, bf16[2,128,1792]{2,1,0:T(8,128)(2,1)S(1)}, u32[]{:S(2)}, u32[]{:S(2)}) %collective-permute-start.86) | collective-permute-done | bytes 917536 | tf_op jit(solution)/shard_map/ppermute | solution.py:23
  661.0 9.6 %collective-permute-done.88.refs_9_.refs_10_ = bf16[2,128,1792]{2,1,0:T(8,128)(2,1)S(1)} collective-permute-done((bf16[2,128,1792]{2,1,0:T(8,128)(2,1)}, bf16[2,128,1792]{2,1,0:T(8,128)(2,1)S(1)}, u32[]{:S(2)}, u32[]{:S(2)}) %collective-permute-start.88) | collective-permute-done | bytes 917536 | tf_op jit(solution)/shard_map/ppermute | solution.py:23
  718.3 9.0 collective-permute-start.98
  739.7 9.5 %collective-permute-done.100.refs_9_.refs_10_ = bf16[2,128,1792]{2,1,0:T(8,128)(2,1)S(1)} collective-permute-done((bf16[2,128,1792]{2,1,0:T(8,128)(2,1)}, bf16[2,128,1792]{2,1,0:T(8,128)(2,1)S(1)}, u32[]{:S(2)}, u32[]{:S(2)}) %collective-permute-start.100) | collective-permute-done | bytes 917536 | tf_op jit(solution)/shard_map/ppermute | solution.py:23
  777.3 8.9 collective-permute-start.113
  798.7 9.6 %collective-permute-done.115.refs_9_.refs_10_ = bf16[2,128,1792]{2,1,0:T(8,128)(2,1)} collective-permute-done((bf16[2,128,1792]{2,1,0:T(8,128)(2,1)}, bf16[2,128,1792]{2,1,0:T(8,128)(2,1)}, u32[]{:S(2)}, u32[]{:S(2)}) %collective-permute-start.115) | collective-permute-done | bytes 917536 | tf_op jit(solution)/shard_map/ppermute | solution.py:23
  855.5 11.6 %collective-permute-done.119.refs_4_.refs_5_ = bf16[2,128,1792]{2,1,0:T(8,128)(2,1)S(1)} collective-permute-done((bf16[2,128,1792]{2,1,0:T(8,128)(2,1)S(1)}, bf16[2,128,1792]{2,1,0:T(8,128)(2,1)S(1)}, u32[]{:S(2)}, u32[]{:S(2)}) %collective-permute-start.119) | collective-permute-done | bytes 917536 | tf_op jit(solution)/shard_map/ppermute | solution.py:23
  (705 shorter events, 592.2 us)
Async XLA Ops:
  35.5 36.2 %collective-permute-start.12 = (bf16[1792,256]{1,0:T(8,128)(2,1)S(1)}, bf16[1792,256]{1,0:T(8,128)(2,1)S(1)}, u32[]{:S(2)}, u32[]{:S(2)}) collective-permute-start(bf16[1792,256]{1,0:T(8,128)(2,1)S(1)} %after.1), channel_id=1, source_target_pairs={{8,0},{16,8},{24,16},{28,24},{20,28},{12,20},{4,12},{0,4},{9,1},{1... | collective-permute-start | bytes 2752520 | tf_op jit(solution)/shard_map/ppermute | solution.py:23
  37.4 36.1 %collective-permute-start.11 = (bf16[1792,256]{1,0:T(8,128)(2,1)S(1)}, bf16[1792,256]{1,0:T(8,128)(2,1)S(1)}, u32[]{:S(2)}, u32[]{:S(2)}) collective-permute-start(bf16[1792,256]{1,0:T(8,128)(2,1)S(1)} %after.1), channel_id=1, source_target_pairs={{0,8},{8,16},{16,24},{24,28},{28,20},{20,12},{12,4},{4,0},{1,9},{9... | collective-permute-start | bytes 2752520 | tf_op jit(solution)/shard_map/ppermute | solution.py:23
  52.0 39.3 %collective-permute-start.7 = (bf16[256,1792]{1,0:T(8,128)(2,1)S(1)}, bf16[256,1792]{1,0:T(8,128)(2,1)S(1)}, u32[]{:S(2)}, u32[]{:S(2)}) collective-permute-start(bf16[256,1792]{1,0:T(8,128)(2,1)S(1)} %collective-permute-done.5), channel_id=1, source_target_pairs={{8,0},{16,8},{24,16},{28,24},{20,28},{12,20},{4,12},{0,4},{9,1},{1... | collective-permute-start | bytes 2752520 | tf_op jit(solution)/shard_map/ppermute | solution.py:23
  53.8 39.4 %collective-permute-start.6 = (bf16[256,1792]{1,0:T(8,128)(2,1)S(1)}, bf16[256,1792]{1,0:T(8,128)(2,1)S(1)}, u32[]{:S(2)}, u32[]{:S(2)}) collective-permute-start(bf16[256,1792]{1,0:T(8,128)(2,1)S(1)} %collective-permute-done.4), channel_id=1, source_target_pairs={{0,8},{8,16},{16,24},{24,28},{28,20},{20,12},{12,4},{4,0},{1,9},{9... | collective-permute-start | bytes 2752520 | tf_op jit(solution)/shard_map/ppermute | solution.py:23
  71.7 39.4 %collective-permute-start.14 = (bf16[1792,256]{1,0:T(8,128)(2,1)S(1)}, bf16[1792,256]{1,0:T(8,128)(2,1)}, u32[]{:S(2)}, u32[]{:S(2)}) collective-permute-start(bf16[1792,256]{1,0:T(8,128)(2,1)S(1)} %collective-permute-done.12), channel_id=1, source_target_pairs={{8,0},{16,8},{24,16},{28,24},{20,28},{12,20},{4,12},{0,4},{9,1},{1... | collective-permute-start | bytes 2752520 | tf_op jit(solution)/shard_map/ppermute | solution.py:23
  73.5 39.4 %collective-permute-start.13 = (bf16[1792,256]{1,0:T(8,128)(2,1)S(1)}, bf16[1792,256]{1,0:T(8,128)(2,1)S(1)}, u32[]{:S(2)}, u32[]{:S(2)}) collective-permute-start(bf16[1792,256]{1,0:T(8,128)(2,1)S(1)} %collective-permute-done.11), channel_id=1, source_target_pairs={{0,8},{8,16},{16,24},{24,28},{28,20},{20,12},{12,4},{4,0},{1,9},{9... | collective-permute-start | bytes 2752520 | tf_op jit(solution)/shard_map/ppermute | solution.py:23
  230.2 37.3 %collective-permute-start.32 = (bf16[2,128,1792]{2,1,0:T(8,128)(2,1)}, bf16[2,128,1792]{2,1,0:T(8,128)(2,1)S(1)}, u32[]{:S(2)}, u32[]{:S(2)}) collective-permute-start(bf16[2,128,1792]{2,1,0:T(8,128)(2,1)} %get-tuple-element.148.refs_6_), channel_id=1, source_target_pairs={{8,16},{12,20},{16,8},{20,12},{9,17},{13,21},{17,9},{21,13},{10,18... | collective-permute-start | bytes 2752520 | tf_op jit(solution)/shard_map/ppermute | solution.py:23
  231.9 42.0 %collective-permute-start.36 = (bf16[2,128,1792]{2,1,0:T(8,128)(2,1)S(1)}, bf16[2,128,1792]{2,1,0:T(8,128)(2,1)S(1)}, u32[]{:S(2)}, u32[]{:S(2)}) collective-permute-start(bf16[2,128,1792]{2,1,0:T(8,128)(2,1)S(1)} %tick_across.39.refs_7_), channel_id=1, source_target_pairs={{0,4},{4,0},{8,12},{12,8},{16,20},{20,16},{24,28},{28,24},{1,5},{5... | collective-permute-start | bytes 2752520 | tf_op jit(solution)/shard_map/ppermute | solution.py:23
  237.8 40.1 %collective-permute-start.35 = (bf16[2,128,1792]{2,1,0:T(8,128)(2,1)}, bf16[2,128,1792]{2,1,0:T(8,128)(2,1)S(1)}, u32[]{:S(2)}, u32[]{:S(2)}) collective-permute-start(bf16[2,128,1792]{2,1,0:T(8,128)(2,1)} %get-tuple-element.150.refs_6_), channel_id=1, source_target_pairs={{8,16},{12,20},{16,8},{20,12},{9,17},{13,21},{17,9},{21,13},{10,18... | collective-permute-start | bytes 2752520 | tf_op jit(solution)/shard_map/ppermute | solution.py:23
  238.5 35.4 %collective-permute-start.34 = (bf16[1,128,1792]{2,1,0:T(8,128)(2,1)S(1)}, bf16[1,128,1792]{2,1,0:T(8,128)(2,1)S(1)}, u32[]{:S(2)}, u32[]{:S(2)}) collective-permute-start(bf16[1,128,1792]{2,1,0:T(8,128)(2,1)S(1)} %get-tuple-element.151.refs_1_.refs_6_), channel_id=1, source_target_pairs={{0,8},{4,12},{8,0},{12,4},{16,24},{20,28},{24,16},{28,20},{1,9},{5... | collective-permute-start | bytes 1376264 | tf_op jit(solution)/shard_map/ppermute | solution.py:23
  266.0 36.2 %collective-permute-start.22 = (bf16[192,2048]{1,0:T(8,128)(2,1)S(1)}, bf16[192,2048]{1,0:T(8,128)(2,1)S(1)}, u32[]{:S(2)}, u32[]{:S(2)}) collective-permute-start(bf16[192,2048]{1,0:T(8,128)(2,1)S(1)} %get-tuple-element.139), channel_id=1, source_target_pairs={{0,2},{2,0},{1,3},{3,1},{4,6},{6,4},{5,7},{7,5},{8,10},{10,8},{9,1... | collective-permute-start | bytes 2359304 | tf_op jit(solution)/shard_map/ppermute | solution.py:244
  268.5 45.1 %collective-permute-start.33 = (bf16[2,128,1792]{2,1,0:T(8,128)(2,1)S(1)}, bf16[2,128,1792]{2,1,0:T(8,128)(2,1)S(1)}, u32[]{:S(2)}, u32[]{:S(2)}) collective-permute-start(bf16[2,128,1792]{2,1,0:T(8,128)(2,1)S(1)} %tick_across.40.refs_10_), channel_id=1, source_target_pairs={{0,4},{4,0},{8,12},{12,8},{16,20},{20,16},{24,28},{28,24},{1,5},{5... | collective-permute-start | bytes 2752520 | tf_op jit(solution)/shard_map/ppermute | solution.py:23
  276.8 45.3 %collective-permute-start.38 = (bf16[2,128,1792]{2,1,0:T(8,128)(2,1)S(1)}, bf16[2,128,1792]{2,1,0:T(8,128)(2,1)S(1)}, u32[]{:S(2)}, u32[]{:S(2)}) collective-permute-start(bf16[2,128,1792]{2,1,0:T(8,128)(2,1)S(1)} %get-tuple-element.152.refs_6_), channel_id=1, source_target_pairs={{8,16},{12,20},{16,8},{20,12},{9,17},{13,21},{17,9},{21,13},{10,18... | collective-permute-start | bytes 2752520 | tf_op jit(solution)/shard_map/ppermute | solution.py:23
  278.9 44.3 %collective-permute-start.43 = (bf16[2,128,1792]{2,1,0:T(8,128)(2,1)S(1)}, bf16[2,128,1792]{2,1,0:T(8,128)(2,1)S(1)}, u32[]{:S(2)}, u32[]{:S(2)}) collective-permute-start(bf16[2,128,1792]{2,1,0:T(8,128)(2,1)S(1)} %tick_across.41.refs_11_), channel_id=1, source_target_pairs={{0,4},{4,0},{8,12},{12,8},{16,20},{20,16},{24,28},{28,24},{1,5},{5... | collective-permute-start | bytes 2752520 | tf_op jit(solution)/shard_map/ppermute | solution.py:23
  279.3 34.2 %collective-permute-start.31 = (bf16[1,128,1792]{2,1,0:T(8,128)(2,1)S(1)}, bf16[1,128,1792]{2,1,0:T(8,128)(2,1)S(1)}, u32[]{:S(2)}, u32[]{:S(2)}) collective-permute-start(bf16[1,128,1792]{2,1,0:T(8,128)(2,1)S(1)} %get-tuple-element.149.refs_1_.refs_6_), channel_id=1, source_target_pairs={{0,8},{4,12},{8,0},{12,4},{16,24},{20,28},{24,16},{28,20},{1,9},{5... | collective-permute-start | bytes 1376264 | tf_op jit(solution)/shard_map/ppermute | solution.py:23
  317.3 32.9 %collective-permute-start.37 = (bf16[2,128,1792]{2,1,0:T(8,128)(2,1)S(1)}, bf16[2,128,1792]{2,1,0:T(8,128)(2,1)S(1)}, u32[]{:S(2)}, u32[]{:S(2)}) collective-permute-start(bf16[2,128,1792]{2,1,0:T(8,128)(2,1)S(1)} %get-tuple-element.153.refs_1_.refs_6_), channel_id=1, source_target_pairs={{0,8},{4,12},{8,0},{12,4},{16,24},{20,28},{24,16},{28,20},{1,9},{5... | collective-permute-start | bytes 2752520 | tf_op jit(solution)/shard_map/ppermute | solution.py:23
  337.3 42.7 %collective-permute-start.47 = (bf16[2,128,1792]{2,1,0:T(8,128)(2,1)}, bf16[2,128,1792]{2,1,0:T(8,128)(2,1)}, u32[]{:S(2)}, u32[]{:S(2)}) collective-permute-start(bf16[2,128,1792]{2,1,0:T(8,128)(2,1)} %get-tuple-element.162.refs_1_.refs_6_), channel_id=1, source_target_pairs={{0,8},{4,12},{8,0},{12,4},{16,24},{20,28},{24,16},{28,20},{1,9},{5... | collective-permute-start | bytes 2752520 | tf_op jit(solution)/shard_map/ppermute | solution.py:23
  399.4 35.2 %collective-permute-start.52 = (bf16[2,128,1792]{2,1,0:T(8,128)(2,1)S(1)}, bf16[2,128,1792]{2,1,0:T(8,128)(2,1)S(1)}, u32[]{:S(2)}, u32[]{:S(2)}) collective-permute-start(bf16[2,128,1792]{2,1,0:T(8,128)(2,1)S(1)} %get-tuple-element.169.refs_10_), channel_id=1, source_target_pairs={{0,4},{4,0},{8,12},{12,8},{16,20},{20,16},{24,28},{28,24},{1,5},{5... | collective-permute-start | bytes 2752520 | tf_op jit(solution)/shard_map/ppermute | solution.py:23
  400.0 34.6 %collective-permute-start.50 = (bf16[2,128,1792]{2,1,0:T(8,128)(2,1)S(1)}, bf16[2,128,1792]{2,1,0:T(8,128)(2,1)S(1)}, u32[]{:S(2)}, u32[]{:S(2)}) collective-permute-start(bf16[2,128,1792]{2,1,0:T(8,128)(2,1)S(1)} %get-tuple-element.166.refs_1_.refs_6_), channel_id=1, source_target_pairs={{0,8},{4,12},{8,0},{12,4},{16,24},{20,28},{24,16},{28,20},{1,9},{5... | collective-permute-start | bytes 2752520 | tf_op jit(solution)/shard_map/ppermute | solution.py:23
  439.0 33.8 %collective-permute-start.56 = (bf16[2,128,1792]{2,1,0:T(8,128)(2,1)}, bf16[2,128,1792]{2,1,0:T(8,128)(2,1)S(1)}, u32[]{:S(2)}, u32[]{:S(2)}) collective-permute-start(bf16[2,128,1792]{2,1,0:T(8,128)(2,1)} %get-tuple-element.174.refs_1_.refs_6_), channel_id=1, source_target_pairs={{0,8},{4,12},{8,0},{12,4},{16,24},{20,28},{24,16},{28,20},{1,9},{5... | collective-permute-start | bytes 2752520 | tf_op jit(solution)/shard_map/ppermute | solution.py:23
  556.6 32.9 %collective-permute-start.74 = (bf16[2,128,1792]{2,1,0:T(8,128)(2,1)}, bf16[2,128,1792]{2,1,0:T(8,128)(2,1)S(1)}, u32[]{:S(2)}, u32[]{:S(2)}) collective-permute-start(bf16[2,128,1792]{2,1,0:T(8,128)(2,1)} %get-tuple-element.198.refs_1_.refs_6_), channel_id=1, source_target_pairs={{0,8},{4,12},{8,0},{12,4},{16,24},{20,28},{24,16},{28,20},{1,9},{5... | collective-permute-start | bytes 2752520 | tf_op jit(solution)/shard_map/ppermute | solution.py:23
  655.1 34.7 %collective-permute-start.95 = (bf16[2,128,1792]{2,1,0:T(8,128)(2,1)}, bf16[2,128,1792]{2,1,0:T(8,128)(2,1)S(1)}, u32[]{:S(2)}, u32[]{:S(2)}) collective-permute-start(bf16[2,128,1792]{2,1,0:T(8,128)(2,1)} %get-tuple-element.226.refs_1_.refs_6_), channel_id=1, source_target_pairs={{0,8},{4,12},{8,0},{12,4},{16,24},{20,28},{24,16},{28,20},{1,9},{5... | collective-permute-start | bytes 2752520 | tf_op jit(solution)/shard_map/ppermute | solution.py:23
  674.7 32.9 %collective-permute-start.92 = (bf16[2,128,1792]{2,1,0:T(8,128)(2,1)}, bf16[2,128,1792]{2,1,0:T(8,128)(2,1)S(1)}, u32[]{:S(2)}, u32[]{:S(2)}) collective-permute-start(bf16[2,128,1792]{2,1,0:T(8,128)(2,1)} %get-tuple-element.222.refs_1_.refs_6_), channel_id=1, source_target_pairs={{0,8},{4,12},{8,0},{12,4},{16,24},{20,28},{24,16},{28,20},{1,9},{5... | collective-permute-start | bytes 2752520 | tf_op jit(solution)/shard_map/ppermute | solution.py:23
  833.2 33.9 %collective-permute-start.119 = (bf16[2,128,1792]{2,1,0:T(8,128)(2,1)S(1)}, bf16[2,128,1792]{2,1,0:T(8,128)(2,1)S(1)}, u32[]{:S(2)}, u32[]{:S(2)}) collective-permute-start(bf16[2,128,1792]{2,1,0:T(8,128)(2,1)S(1)} %get-tuple-element.257.refs_5_), channel_id=1, source_target_pairs={{0,4},{4,0},{8,12},{12,8},{16,20},{20,16},{24,28},{28,24},{1,5},{5... | collective-permute-start | bytes 2752520 | tf_op jit(solution)/shard_map/ppermute | solution.py:23
  (273 other events, 4852.1 us)
